TPU v7x, 32 devices: a whole 2x2x4 slice. The times are simulated.
32 devices in a mesh: snp: 2 (over x), rows: 16 (over z, y, core).
Axes of the slice: x: 2, y: 2, z: 4, core: 2. Of those that a mesh axis runs over, the one named last changes fastest.
Arguments:
- genotypes: float32 [3072, 2560], P('snp', 'rows'), may hold values from -1 to 2, as said below
- relationship: float32 [2560, 2560], P('rows', 'snp'), as said below
Outputs:
- updated: float32 [2560, 2560], P('rows', 'snp')
- panel: float32 [2560, 512], P('rows')
Inputs may be any that keep to these rules, and one draw needn't show every extreme that they name: `genotypes`: expected count of the alternative allele, a real number between 0 and 2; exactly -1 marks a missing call. `relationship`: symmetric.
All inputs are finite; a program needn't handle non-finite values.
Results may differ from a plain program's by a relative error of at most 0.0007.
The roundings to bfloat16 on the way count: a program that leaves them out, or rounds other values in their place, can miss the bound.
Values may be sent and summed in bfloat16 or wider, within the bound.
No kernel may reach another device: no remote copies, remote signals or barrier semaphores. Data moves between devices by JAX's collectives and lax.ppermute only.
A program may use at most 128 MiB of HBM per device.

v0:
```python
import functools

import jax
import jax.numpy as jnp
from jax import lax
from jax.experimental import pallas as pl
from jax.experimental.pallas import tpu as pltpu
from jax.sharding import PartitionSpec as P

PANEL = 512
RIDGE = 0.25
GROUP = 4
BLOCK = 128
SUB = 8

VMEM = pl.BlockSpec(memory_space=pltpu.VMEM)
SMEM = pl.BlockSpec(memory_space=pltpu.SMEM)
ANYWHERE = pl.BlockSpec(memory_space=pl.ANY)


def precise(a, b, contract):
    return lax.dot_general(
        a,
        b,
        (((1,), (contract,)), ((), ())),
        precision=lax.Precision.HIGHEST,
        preferred_element_type=jnp.float32,
    )


def times(a, b):
    return lax.dot_general(
        a, b, (((1,), (1,)), ((), ())), preferred_element_type=jnp.float32
    )


def split(x):
    high = x.astype(jnp.bfloat16)
    return high, (x - high.astype(jnp.float32)).astype(jnp.bfloat16)


def cost(flops):
    return pl.CostEstimate(flops=flops, bytes_accessed=131072, transcendentals=0)


def room(*arrays):
    total = sum(x.size * x.dtype.itemsize for x in arrays)
    return pltpu.CompilerParams(vmem_limit_bytes=total * 3 // 2 + 3 * 2**20)


def f32(*shape):
    return jax.ShapeDtypeStruct(shape, jnp.float32)


def invert_factor(work):
    lane = lax.broadcasted_iota(jnp.int32, (SUB, BLOCK), 1)
    for g in range(BLOCK // SUB):
        at = g * SUB
        own = work[at : at + SUB, :]
        inside = (lane >= at) & (lane < at + SUB)
        rows = [jnp.broadcast_to(own[u : u + 1, :], (SUB, BLOCK)) for u in range(SUB)]
        e = [
            [
                jnp.broadcast_to(rows[t][:, at + u : at + u + 1], (SUB, BLOCK))
                for t in range(u + 1)
            ]
            for u in range(SUB)
        ]
        rows = [
            jnp.where(inside, jnp.where(lane == at + u, 1.0, 0.0), rows[u])
            for u in range(SUB)
        ]
        low = [[None] * SUB for _ in range(SUB)]
        scale = []
        for t in range(SUB):
            r = lax.rsqrt(e[t][t])
            scale.append(r)
            for u in range(t + 1, SUB):
                low[u][t] = e[u][t] * r
            for u in range(t + 1, SUB):
                for v in range(t + 1, u + 1):
                    e[u][v] = e[u][v] - low[u][t] * low[v][t]
            rows[t] = rows[t] * r
            for u in range(t + 1, SUB):
                rows[u] = rows[u] - low[u][t] * rows[t]
        for below in range(g + 1, BLOCK // SUB):
            base = below * SUB
            rest = work[base : base + SUB, :]
            c = [
                jnp.broadcast_to(rest[:, at + t : at + t + 1], (SUB, BLOCK))
                for t in range(SUB)
            ]
            rest = jnp.where(inside, 0.0, rest)
            for t in range(SUB):
                c[t] = c[t] * scale[t]
                for s in range(t + 1, SUB):
                    c[s] = c[s] - low[s][t] * c[t]
                rest = rest - c[t] * rows[t]
            work[base : base + SUB, :] = rest
        for t in range(SUB):
            work[at + t : at + t + 1, :] = rows[t][0:1, :]


def in_order(place, blocks, out):
    rows = blocks[0].shape[0]
    for k in range(GROUP):
        start = pl.multiple_of((place[0] ^ k) * rows, 16)
        out[pl.ds(start, rows), :] = blocks[k][...]


def factor_step_kernel(size, n_in, *refs):
    place, squares = refs[0], refs[1 : 1 + n_in]
    if size > BLOCK:
        inverse, column, rest, work = refs[-4:]
    else:
        inverse, work = refs[-2:]
    if n_in == 1:
        square = squares[0]
    else:
        square = rest_in = refs[-5]
        in_order(place, squares, rest_in)
    work[...] = square[:BLOCK, :BLOCK]
    invert_factor(work)
    i = lax.broadcasted_iota(jnp.int32, (BLOCK, BLOCK), 0)
    j = lax.broadcasted_iota(jnp.int32, (BLOCK, BLOCK), 1)
    value = jnp.where(j <= i, work[...], 0.0)
    inverse[...] = value
    if size > BLOCK:
        below = precise(square[BLOCK:size, :BLOCK], value, 1)
        column[...] = below
        for n in range(size // BLOCK - 1):
            cut = slice(n * BLOCK, size - BLOCK)
            across = slice(n * BLOCK, (n + 1) * BLOCK)
            rest[cut, across] = square[
                (n + 1) * BLOCK : size, (n + 1) * BLOCK : (n + 2) * BLOCK
            ] - precise(below[n * BLOCK :, :], below[across, :], 1)


def factor_step(place, squares, size, waits):
    left = size - BLOCK
    out_shape = [f32(BLOCK, BLOCK)]
    scratch = [pltpu.VMEM((BLOCK, BLOCK), jnp.float32)]
    if left:
        out_shape += [f32(left, BLOCK), f32(left, left)]
    n_in = len(squares)
    kernel = functools.partial(factor_step_kernel, size, n_in)
    if n_in > 1:

        def kernel(*refs):
            *others, work, whole = refs
            outs = 3 if left else 1
            return factor_step_kernel(
                size, n_in, *others[:-outs], whole, *others[-outs:], work
            )

        scratch.append(pltpu.VMEM((GROUP * squares[0].shape[0], size), jnp.float32))
    return pl.pallas_call(
        kernel,
        out_shape=out_shape,
        in_specs=[SMEM] + [VMEM] * n_in + [ANYWHERE] * len(waits),
        out_specs=[VMEM] * len(out_shape),
        scratch_shapes=scratch,
        compiler_params=room(*out_shape, f32(2 * size, size), *squares),
        cost_estimate=cost(6_000_000_000),
    )(place, *squares, *waits)


def solve_kernel(blocks, columns, *refs):
    inverses, below = refs[:blocks], refs[blocks : 2 * blocks - 1]
    panel, weights = refs[-2:]
    found = []
    for k in range(blocks):
        total = columns[:, k * BLOCK : (k + 1) * BLOCK]
        for j in range(k):
            start = (k - j - 1) * BLOCK
            total = total - precise(found[j], below[j][start : start + BLOCK, :], 1)
        found.append(precise(total, inverses[k][...], 1))
        panel[:, k * BLOCK : (k + 1) * BLOCK] = found[k]
    for k in reversed(range(blocks)):
        total = found[k]
        for j in range(k + 1, blocks):
            start = (j - k - 1) * BLOCK
            total = total - precise(found[j], below[k][start : start + BLOCK, :], 0)
        found[k] = precise(total, inverses[k][...], 0)
        weights[:, k * BLOCK : (k + 1) * BLOCK] = found[k]


def solve(columns, inverses, below):
    own = columns.shape[0]
    return pl.pallas_call(
        functools.partial(solve_kernel, len(inverses)),
        out_shape=[f32(own, PANEL), f32(own, PANEL)],
        in_specs=[VMEM] * (2 * len(inverses)),
        out_specs=[VMEM, VMEM],
        compiler_params=room(columns, columns, columns, *inverses, *below),
        cost_estimate=cost(4 * own * PANEL * PANEL),
    )(columns, *inverses, *below)


def head_kernel(n_left, sizes, place, *refs):
    left, head = refs[:n_left], refs[n_left : n_left + GROUP]
    outs, order = refs[-1 - len(sizes) : -1], refs[-1]
    own = head[0].shape[0]
    in_order(place, head, order)
    at = 0
    for out, count in zip(outs, sizes):
        for n in range(count):
            out[n * own : (n + 1) * own, :] = times(left[at][...], order[:PANEL, :])
            at += 1


def head_products(place, groups, head, waits):
    own = head[0].shape[0]
    left = [x for group in groups for x in group]
    sizes = [len(group) for group in groups]
    return pl.pallas_call(
        functools.partial(head_kernel, len(left), sizes),
        out_shape=[f32(n * own, PANEL) for n in sizes],
        in_specs=[SMEM] + [VMEM] * (len(left) + GROUP) + [ANYWHERE] * len(waits),
        out_specs=[VMEM] * len(sizes),
        scratch_shapes=[pltpu.VMEM((GROUP * own, head[0].shape[1]), head[0].dtype)],
        compiler_params=room(*left, *head, *head, f32(len(left) * own, PANEL)),
        cost_estimate=cost(2 * len(left) * own * PANEL * head[0].shape[1]),
    )(place, *left, *head, *waits)


def gram_kernel(n_cols, n_more, *refs):
    plane, cols = refs[:GROUP], refs[GROUP : GROUP + n_cols]
    more = refs[GROUP + n_cols : GROUP + n_cols + n_more]
    outs = refs[-GROUP:]
    own = plane[0].shape[0]
    for k in range(GROUP):
        for j in range(n_cols):
            product = times(cols[j][...], plane[k][...])
            across = slice(j * own, (j + 1) * own)
            for x in more:
                product = product + x[across, k * own : (k + 1) * own]
            outs[k][:, across] = product.T


def gram_out_kernel(n_cols, *refs):
    plane, cols, out = refs[:GROUP], refs[GROUP : GROUP + n_cols], refs[-1]
    own = plane[0].shape[0]
    for k in range(GROUP):
        for j in range(n_cols):
            out[j * own : (j + 1) * own, k * own : (k + 1) * own] = times(
                cols[j][...], plane[k][...]
            )


def gram_products(plane, cols, more, waits):
    own, depth = plane[0].shape
    width = len(cols) * own
    if more is None:
        kernel = functools.partial(gram_out_kernel, len(cols))
        out_shape, out_specs, more = f32(width, GROUP * own), VMEM, []
    else:
        kernel = functools.partial(gram_kernel, len(cols), len(more))
        out_shape, out_specs = [f32(own, width)] * GROUP, [VMEM] * GROUP
    return pl.pallas_call(
        kernel,
        out_shape=out_shape,
        in_specs=[VMEM] * (GROUP + len(cols) + len(more))
        + [ANYWHERE] * len(waits),
        out_specs=out_specs,
        compiler_params=room(*plane, *cols, *more, f32(GROUP * own, width)),
        cost_estimate=cost(2 * GROUP * own * width * depth),
    )(*plane, *cols, *more, *waits)


def update_kernel(own, part, place, scale, rel, weights, *refs):
    pieces, sides = refs[:GROUP], refs[GROUP : 2 * GROUP]
    out, all_pieces, all_sides = refs[2 * GROUP :]
    in_order(place, pieces, all_pieces)
    in_order(place, sides, all_sides)
    i = lax.broadcasted_iota(jnp.int32, (own, own), 0)
    j = lax.broadcasted_iota(jnp.int32, (own, own), 1)
    ridge = jnp.where(i == j, RIDGE, 0.0)
    high, low = split(weights[...])
    width = part * own
    for m in range(GROUP):
        side_high, side_low = split(all_sides[m * width : (m + 1) * width, :])
        product = times(high, side_low) + times(low, side_high)
        product = product + times(high, side_high)
        for n in range(part):
            at = (n * GROUP + m) * own
            cut = slice(n * own, (n + 1) * own)
            here = (place[0] == m) & (place[1] == n)
            value = rel[:, at : at + own] - product[:, cut]
            value = value + all_pieces[m * own : (m + 1) * own, cut] * scale[0]
            out[:, at : at + own] = value + ridge * jnp.where(here, 1.0, 0.0)


def final_update(place, scale, rel, weights, pieces, sides):
    own, width = rel.shape
    part = width // (GROUP * own)
    return pl.pallas_call(
        functools.partial(update_kernel, own, part),
        out_shape=f32(own, width),
        in_specs=[SMEM, SMEM] + [VMEM] * (2 + 2 * GROUP),
        out_specs=VMEM,
        scratch_shapes=[
            pltpu.VMEM((GROUP * own, part * own), jnp.float32),
            pltpu.VMEM((width, PANEL), jnp.float32),
        ],
        compiler_params=room(rel, rel, weights, *pieces, *pieces, *sides, *sides),
        cost_estimate=cost(2 * own * width * PANEL),
    )(place, scale, rel, weights, *pieces, *sides)


def nothing(*refs):
    pass


def after(x, *done):
    return pl.pallas_call(
        nothing,
        out_shape=jax.ShapeDtypeStruct(x.shape, x.dtype),
        in_specs=[ANYWHERE] * (1 + len(done)),
        out_specs=ANYWHERE,
        input_output_aliases={0: 0},
        compiler_params=pltpu.CompilerParams(vmem_limit_bytes=2**20),
    )(x, *done)


def select_order(blocks, member):
    bit = 1
    while bit < len(blocks):
        swap = (member & bit) != 0
        blocks = [
            jnp.where(swap, blocks[k ^ bit], blocks[k]) for k in range(len(blocks))
        ]
        bit *= 2
    return blocks


def make(n_rows, n_snp):
    lines = n_rows // GROUP
    part = lines // n_snp
    far = lines // 2

    def rows_xor(x, bits):
        return lax.ppermute(x, "rows", [(r, r ^ bits) for r in range(n_rows)])

    def snp_xor(x, bits):
        return lax.ppermute(x, "snp", [(s, s ^ bits) for s in range(n_snp)])

    def from_first_snp(x, rank):
        got = x
        for s in range(1, n_snp):
            got = jnp.where(rank == s, lax.ppermute(x, "snp", [(0, s)]), got)
        return got

    def group_gather(x):
        core = rows_xor(x, 1)
        other = rows_xor(x, 2)
        return [x, core, other, rows_xor(other, 1)]

    def line_gather(x, hold):
        near = {k: rows_xor(x, k * GROUP) for k in range(1, far)}
        passed = hold(rows_xor(x, far * GROUP), list(near.values()))
        parts = {0: x, far: passed, **near}
        for k in range(1, far):
            parts[far + k] = rows_xor(passed, k * GROUP)
        return [parts[k] for k in range(lines)]

    def rows_sum(x):
        bit = 1
        while bit < n_rows:
            if bit * 2 < n_rows:
                parts = [x] + [rows_xor(x, bit * k) for k in (1, 2, 3)]
                x = (parts[0] + parts[1]) + (parts[2] + parts[3])
                bit *= 4
            else:
                x = x + rows_xor(x, bit)
                bit *= 2
        return x

    def snp_sum(x):
        bit = 1
        while bit < n_snp:
            x = x + snp_xor(x, bit)
            bit *= 2
        return x

    def per_device(genotypes, relationship):
        own = genotypes.shape[1]
        rank = lax.axis_index("rows")
        col = lax.axis_index("snp")
        q = rank % GROUP
        z = rank // GROUP
        place = jnp.stack([q, z - col * part]).astype(jnp.int32)

        called = genotypes >= 0
        dosage = jnp.where(called, genotypes, 0.0)
        stats = jnp.stack(
            [jnp.sum(dosage, axis=1), jnp.sum(called.astype(jnp.float32), axis=1)]
        )
        stats = rows_sum(stats)
        frequency = stats[0] / (2.0 * stats[1])
        scale_part = jnp.sum(2.0 * frequency * (1.0 - frequency))
        gt = lax.optimization_barrier(genotypes.T)
        centered = jnp.where(gt >= 0, gt - 2.0 * frequency[None, :], 0.0).astype(
            jnp.bfloat16
        )

        rel_own = from_first_snp(relationship[:, :PANEL], col)
        ids = rank * own + lax.broadcasted_iota(jnp.int32, rel_own.shape, 0)
        rel_own = rel_own + jnp.where(
            ids == lax.broadcasted_iota(jnp.int32, rel_own.shape, 1), RIDGE, 0.0
        )

        core, other = rows_xor(centered, 1), rows_xor(centered, 2)
        line = line_gather(centered, lambda x, near: after(x, rel_own, *near))
        line[-1] = after(line[-1], other)
        plane = [centered, core, other, rows_xor(other, 1)]
        first = select_order(line, z)[0]
        member = after((z ^ (col * part)).astype(jnp.int32).reshape(1), first)[0]
        ordered = select_order(line, member)
        groups = [ordered[bits * part : (bits + 1) * part] for bits in range(n_snp)]
        rel_line = line_gather(after(rel_own, line[-1]), lambda x, near: x)

        leaving = [gram_products(plane, groups[b], None, []) for b in range(1, n_snp)]

        head = [first, rows_xor(first, 1)]
        head.append(after(rows_xor(first, 2), *rel_line[1 : far + 1], *leaving))
        head.append(rows_xor(head[2], 1))
        (rows,) = head_products(place, [[first]], head, [])
        rows = jnp.concatenate(
            [rows, jnp.broadcast_to(scale_part.reshape(1, 1), (SUB, PANEL))], axis=0
        )
        total = snp_sum(rows)
        inverse = 1.0 / total[own, 0]
        total = total[:own] * inverse + select_order(rel_line, z)[0]
        sides = head_products(place, groups, head, [rows])
        total = after(total, *sides[1:])
        side_got = [snp_xor(sides[bits], bits) for bits in range(1, n_snp)]

        (lead,) = head_products(place, [[centered]], head, [total])
        diagonal = [total, rows_xor(total, 1)]
        diagonal.append(after(rows_xor(total, 2), lead))
        diagonal.append(rows_xor(diagonal[2], 1))

        gram_got = [
            snp_xor(after(leaving[b - 1], *side_got), b) for b in range(1, n_snp)
        ]
        pieces = gram_products(plane, groups[0], gram_got, [])
        moved = [pieces[0]] + [rows_xor(pieces[k], k) for k in range(1, GROUP)]

        inv, column, square = factor_step(place, diagonal, PANEL, side_got)
        inverses, below = [inv], [column]
        side = sides[0]
        for got in side_got:
            side = side + after(got, inverses[0])
        rel_side = select_order(rel_line, z ^ (col * part))[:part]
        side = jnp.concatenate(
            [
                rel_side[j] + side[j * own : (j + 1) * own] * inverse
                for j in range(part)
            ],
            axis=0,
        )
        sides = [side, rows_xor(side, 1), rows_xor(side, 2)]

        waits = [[], [side], [pieces[1]], []]
        for k in range(1, PANEL // BLOCK):
            inv, *more = factor_step(place, [square], PANEL - k * BLOCK, waits[k])
            inverses.append(inv)
            if more:
                column, square = more
                below.append(column)

        sides[2] = after(sides[2], inverses[2])
        sides.append(rows_xor(sides[2], 1))

        own_columns = rel_own + snp_sum(after(lead, pieces[1])) * inverse
        panel, weights = solve(own_columns, inverses, below)
        updated = final_update(
            place, inverse.reshape(1), relationship, weights, moved, sides
        )
        return updated, panel

    return per_device


def solution(mesh):
    return jax.shard_map(
        make(mesh.shape["rows"], mesh.shape["snp"]),
        mesh=mesh,
        in_specs=(P("snp", "rows"), P("rows", "snp")),
        out_specs=(P("rows", "snp"), P("rows", None)),
        check_vma=False,
    )
```

profile of v0, /device:TPU:0, one launch (start us, length us, event | category | flops | bytes accessed | tf_op | source)
XLA Modules:
  0.0 145.5 jit_solution(16957007453380413780)
XLA Ops:
  2.7 2.6 %collective-permute-start.1 = (f32[2,1536]{1,0:T(2,128)S(1)}, f32[2,1536]{1,0:T(2,128)S(1)}, u32[]{:S(2)}, u32[]{:S(2)}) collective-permute-start(f32[2,1536]{1,0:T(2,128)S(1)} %pad_maximum_fusion.1), channel_id=1, source_target_pairs={{0,2},{1,3},{2,0},{3,1},{4,6},{5,7},{6,4},{7,5},{8,10},{9,11},{10,... | collective-permute-start | bytes 36872 | tf_op jit(solution)/shard_map/ppermute | solution.py:343
  10.1 2.6 %collective-permute-start.4 = (f32[2,1536]{1,0:T(2,128)S(1)}, f32[2,1536]{1,0:T(2,128)S(1)}, u32[]{:S(2)}, u32[]{:S(2)}) collective-permute-start(f32[2,1536]{1,0:T(2,128)S(1)} %add_add_fusion.1), channel_id=1, source_target_pairs={{0,8},{1,9},{2,10},{3,11},{4,12},{5,13},{6,14},{7,15},{8,0},{9,1},... | collective-permute-start | bytes 36872 | tf_op jit(solution)/shard_map/ppermute | solution.py:343
  13.0 3.4 %collective-permute-start.7 = (f32[160,512]{1,0:T(8,128)S(1)}, f32[160,512]{1,0:T(8,128)S(1)}, u32[]{:S(2)}, u32[]{:S(2)}) collective-permute-start(f32[160,512]{1,0:T(8,128)S(1)} %slice.23), channel_id=1, source_target_pairs={{0,16},{1,17},{2,18},{3,19},{4,20},{5,21},{6,22},{7,23},{8,24},{9,... | collective-permute-start | bytes 983048 | tf_op jit(solution)/shard_map/ppermute | solution.py:351
  16.4 1.8 %collective-permute-done.5 = f32[2,1536]{1,0:T(2,128)S(1)} collective-permute-done((f32[2,1536]{1,0:T(2,128)S(1)}, f32[2,1536]{1,0:T(2,128)S(1)}, u32[]{:S(2)}, u32[]{:S(2)}) %collective-permute-start.5) | collective-permute-done | bytes 12320 | tf_op jit(solution)/shard_map/ppermute | solution.py:343
  19.1 2.4 %collective-permute-start.6 = (bf16[160,1536]{1,0:T(8,128)(2,1)S(1)}, bf16[160,1536]{1,0:T(8,128)(2,1)S(1)}, u32[]{:S(2)}, u32[]{:S(2)}) collective-permute-start(bf16[160,1536]{1,0:T(8,128)(2,1)S(1)} %select_convert_fusion.refs_0_), channel_id=1, source_target_pairs={{0,8},{1,9},{2,10},{3,11},{4,12},{5,13},{6,14},{7,15},{8,0},{9,1},... | collective-permute-start | bytes 1474568 | tf_op jit(solution)/shard_map/ppermute | solution.py:343
  23.0 18.0 %collective-permute-done.8.refs_2_ = bf16[160,1536]{1,0:T(8,128)(2,1)S(1)} collective-permute-done((bf16[160,1536]{1,0:T(8,128)(2,1)S(1)}, bf16[160,1536]{1,0:T(8,128)(2,1)S(1)}, u32[]{:S(2)}, u32[]{:S(2)}) %collective-permute-start.8) | collective-permute-done | bytes 491552 | tf_op jit(solution)/shard_map/ppermute | solution.py:343
  43.2 10.4 %collective-permute-done.9.refs_0_ = bf16[160,1536]{1,0:T(8,128)(2,1)S(1)} collective-permute-done((bf16[160,1536]{1,0:T(8,128)(2,1)S(1)}, bf16[160,1536]{1,0:T(8,128)(2,1)S(1)}, u32[]{:S(2)}, u32[]{:S(2)}) %collective-permute-start.9) | collective-permute-done | bytes 491552 | tf_op jit(solution)/shard_map/ppermute | solution.py:343
  54.0 6.2 %collective-permute-start.14 = (f32[160,512]{1,0:T(8,128)S(1)}, f32[160,512]{1,0:T(8,128)}, u32[]{:S(2)}, u32[]{:S(2)}) collective-permute-start(f32[160,512]{1,0:T(8,128)S(1)} %shard_map.43), channel_id=1, source_target_pairs={{0,8},{1,9},{2,10},{3,11},{4,12},{5,13},{6,14},{7,15},{8,0},{9,1},... | collective-permute-start | bytes 983048 | tf_op jit(solution)/shard_map/ppermute | solution.py:343
  63.0 2.3 %broadcast_select_fusion.4 = (bf16[160,1536]{1,0:T(8,128)(2,1)}, bf16[160,1536]{1,0:T(8,128)(2,1)S(1)}, bf16[160,1536]{1,0:T(8,128)(2,1)}, bf16[160,1536]{1,0:T(8,128)(2,1)S(1)}) fusion(pred[]{:T(512)} %bitcast.4, bf16[160,1536]{1,0:T(8,128)(2,1)S(1)} %copy-done.16, pred[]{:T(512)} %bitcast.5, bf16[160,1536]{1,0:T(8,128)(2,1)} %copy-done.17, ...), kind=kLoop, calls=%fused_computation.11 | loop fusion | flops 2949120 | bytes 4429826 | tf_op jit(solution)/shard_map/jit(_where)/select_n | solution.py:331
  65.4 2.7 %shard_map.45.refs_3_.refs_0_ = f32[320,640]{1,0:T(8,128)S(1)} custom-call(bf16[160,1536]{1,0:T(8,128)(2,1)S(1)} %select_convert_fusion.refs_0_, bf16[160,1536]{1,0:T(8,128)(2,1)S(1)} %collective-permute-done.15.refs_1_, bf16[160,1536]{1,0:T(8,128)(2,1)} %collective-permute-done.10.refs_1_.refs_2_, bf16[160,1536]{1,0:T(8,128)(2,1)S(1)} %collective-permute-done.16.refs_3_, ...), custom_call_target="tpu_custom_call" | custom-call | flops 629145600 | bytes 131072 | tf_op jit(solution)/shard_map/pallas_call | solution.py:260
  71.3 2.0 %shard_map.47 = f32[160,512]{1,0:T(8,128)S(1)} custom-call(s32[2]{0:T(128)S(1)} %pad_add_fusion.place.refs_0_, bf16[160,1536]{1,0:T(8,128)(2,1)S(1)} %select_select_fusion.refs_1_.refs_0_.refs_4_, bf16[160,1536]{1,0:T(8,128)(2,1)S(1)} %select_select_fusion.refs_1_.refs_0_.refs_4_, bf16[160,1536]{1,0:T(8,128)(2,1)} %collective-permute-done.11.refs_2_.refs_5_, ...), custom_call_target="tpu_custom_call" | custom-call | flops 251658240 | bytes 131072 | tf_op jit(solution)/shard_map/pallas_call | solution.py:216
  75.5 4.2 %shard_map.48 = (f32[320,512]{1,0:T(8,128)S(1)}, f32[320,512]{1,0:T(8,128)}) custom-call(s32[2]{0:T(128)S(1)} %pad_add_fusion.place.refs_0_, bf16[160,1536]{1,0:T(8,128)(2,1)S(1)} %copy-done.7, bf16[160,1536]{1,0:T(8,128)(2,1)S(1)} %copy-done.5, bf16[160,1536]{1,0:T(8,128)(2,1)S(1)} %copy-done.14, bf16[160,1536]{1,0:T(8,128)(2,1)S(1)} %copy-done.12, ...), custom_call_target="tpu_custom_call" | custom-call | flops 1006632960 | bytes 131072 | tf_op jit(solution)/shard_map/pallas_call | solution.py:216
  80.5 4.6 %collective-permute-done.18 = f32[168,512]{1,0:T(8,128)S(1)} collective-permute-done((f32[168,512]{1,0:T(8,128)S(1)}, f32[168,512]{1,0:T(8,128)S(1)}, u32[]{:S(2)}, u32[]{:S(2)}) %collective-permute-start.18) | collective-permute-done | bytes 344096 | tf_op jit(solution)/shard_map/ppermute | solution.py:346
  87.1 2.0 %fusion.4.refs_0_ = f32[160,512]{1,0:T(8,128)} fusion(f32[168,512]{1,0:T(8,128)S(1)} %pad_add_fusion.1, f32[160,512]{1,0:T(8,128)S(1)} %copy-done.19, f32[160,512]{1,0:T(8,128)S(1)} %copy-done.3, f32[160,512]{1,0:T(8,128)S(1)} %collective-permute-done.19, f32[160,512]{1,0:T(8,128)} %collective-permute-done.14.refs_2_, f32[]{:T(128)} %bitcast.7, pred[]{:T(512)S(6)} %ne.41, ...), kind=kLoop, calls=%fused_computation.20 | loop fusion | flops 409600 | bytes 1966086 | tf_op jit(solution)/shard_map/add | solution.py:434
  90.1 1.8 %shard_map.50.refs_0_.refs_1_ = f32[160,512]{1,0:T(8,128)S(1)} custom-call(s32[2]{0:T(128)S(1)} %pad_add_fusion.place.refs_0_, bf16[160,1536]{1,0:T(8,128)(2,1)S(1)} %select_convert_fusion.refs_0_, bf16[160,1536]{1,0:T(8,128)(2,1)S(1)} %select_select_fusion.refs_1_.refs_0_.refs_4_, bf16[160,1536]{1,0:T(8,128)(2,1)} %collective-permute-done.11.refs_2_.refs_5_, ...), custom_call_target="tpu_custom_call" | custom-call | flops 251658240 | bytes 131072 | tf_op jit(solution)/shard_map/pallas_call | solution.py:216
  92.0 5.6 %collective-permute-done.24.refs_0_ = f32[160,512]{1,0:T(8,128)} collective-permute-done((f32[160,512]{1,0:T(8,128)}, f32[160,512]{1,0:T(8,128)}, u32[]{:S(2)}, u32[]{:S(2)}) %collective-permute-start.24) | collective-permute-done | bytes 327712 | tf_op jit(solution)/shard_map/ppermute | solution.py:343
  101.3 6.8 %shard_map.55 = (f32[128,128]{1,0:T(8,128)S(1)}, f32[384,128]{1,0:T(8,128)S(1)}, f32[384,384]{1,0:T(8,128)S(1)}) custom-call(s32[2]{0:T(128)S(1)} %pad_add_fusion.place.refs_0_, f32[160,512]{1,0:T(8,128)} %shard_map.49.refs_5_.refs_1_, f32[160,512]{1,0:T(8,128)} %collective-permute-done.23.refs_2_, f32[160,512]{1,0:T(8,128)} %shard_map.54.refs_3_, ...), custom_call_target="tpu_custom_call" | custom-call | flops 6000000000 | bytes 131072 | tf_op jit(solution)/shard_map/pallas_call | solution.py:157
  112.8 5.9 %shard_map.57 = (f32[128,128]{1,0:T(8,128)S(1)}, f32[256,128]{1,0:T(8,128)S(1)}, f32[256,256]{1,0:T(8,128)S(1)}) custom-call(s32[2]{0:T(128)S(1)} %pad_add_fusion.place.refs_0_, f32[384,384]{1,0:T(8,128)S(1)} %get-tuple-element.22.refs_1_, f32[320,512]{1,0:T(8,128)S(1)} %pad_maximum_fusion.refs_2_.refs_4_), custom_call_target="tpu_custom_call" | custom-call | flops 6000000000 | bytes 131072 | tf_op jit(solution)/shard_map/pallas_call | solution.py:157
  118.8 2.5 %shard_map.52 = (f32[160,320]{1,0:T(8,128)S(1)}, f32[160,320]{1,0:T(8,128)S(1)}, f32[160,320]{1,0:T(8,128)S(1)}, f32[160,320]{1,0:T(8,128)S(1)}) custom-call(bf16[160,1536]{1,0:T(8,128)(2,1)S(1)} %select_convert_fusion.refs_0_, bf16[160,1536]{1,0:T(8,128)(2,1)S(1)} %copy-done.24, bf16[160,1536]{1,0:T(8,128)(2,1)} %collective-permute-done.10.refs_1_.refs_2_, ...), custom_call_target="tpu_custom_call" | custom-call | flops 629145600 | bytes 131072 | tf_op jit(solution)/shard_map/pallas_call | solution.py:260
  124.0 5.7 %shard_map.58 = (f32[128,128]{1,0:T(8,128)S(1)}, f32[128,128]{1,0:T(8,128)S(1)}, f32[128,128]{1,0:T(8,128)S(1)}) custom-call(s32[2]{0:T(128)S(1)} %pad_add_fusion.place.refs_0_, f32[256,256]{1,0:T(8,128)S(1)} %get-tuple-element.25.refs_1_, f32[160,320]{1,0:T(8,128)S(1)} %get-tuple-element.20.refs_1_.refs_2_), custom_call_target="tpu_custom_call" | custom-call | flops 6000000000 | bytes 131072 | tf_op jit(solution)/shard_map/pallas_call | solution.py:157
  129.8 4.5 %shard_map.59.refs_3_ = f32[128,128]{1,0:T(8,128)S(1)} custom-call(s32[2]{0:T(128)S(1)} %pad_add_fusion.place.refs_0_, f32[128,128]{1,0:T(8,128)S(1)} %get-tuple-element.27.refs_1_), custom_call_target="tpu_custom_call" | custom-call | flops 6000000000 | bytes 131072 | tf_op jit(solution)/shard_map/pallas_call | solution.py:157
  135.2 4.4 %shard_map.60 = (f32[160,512]{1,0:T(8,128)}, f32[160,512]{1,0:T(8,128)S(1)}) custom-call(f32[160,512]{1,0:T(8,128)S(1)} %multiply_add_fusion.columns, f32[128,128]{1,0:T(8,128)S(1)} %get-tuple-element.21.refs_1_.refs_0_, f32[128,128]{1,0:T(8,128)S(1)} %get-tuple-element.24.refs_1_, f32[128,128]{1,0:T(8,128)S(1)} %get-tuple-element.26.refs_2_.refs_1_, ...), custom_call_target="tpu_custom_call" | custom-call | flops 167772160 | bytes 131072 | tf_op jit(solution)/shard_map/pallas_call | solution.py:190
  139.6 2.4 %collective-permute-done.28.refs_3_ = f32[160,320]{1,0:T(8,128)S(1)} collective-permute-done((f32[160,320]{1,0:T(8,128)S(1)}, f32[160,320]{1,0:T(8,128)S(1)}, u32[]{:S(2)}, u32[]{:S(2)}) %collective-permute-start.28) | collective-permute-done | bytes 204832 | tf_op jit(solution)/shard_map/ppermute | solution.py:343
  142.0 3.4 %shard_map.62 = f32[160,1280]{1,0:T(8,128)} custom-call(s32[2]{0:T(128)S(1)} %pad_add_fusion.place.refs_0_, f32[1]{0:T(128)} %bitcast.6.scale, f32[160,1280]{1,0:T(8,128)S(1)} %copy-done.22, f32[160,512]{1,0:T(8,128)S(1)} %get-tuple-element.31.weights, f32[160,320]{1,0:T(8,128)S(1)} %get-tuple-element.32.refs_0_, ...), custom_call_target="tpu_custom_call" | custom-call | flops 209715200 | bytes 131072 | tf_op jit(solution)/shard_map/pallas_call | solution.py:297
  (155 shorter events, 34.0 us)
Async XLA Ops:
  8.5 7.9 %collective-permute-start.3 = (f32[2,1536]{1,0:T(2,128)S(1)}, f32[2,1536]{1,0:T(2,128)S(1)}, u32[]{:S(2)}, u32[]{:S(2)}) collective-permute-start(f32[2,1536]{1,0:T(2,128)S(1)} %add_add_fusion.1), channel_id=1, source_target_pairs={{0,4},{1,5},{2,6},{3,7},{4,0},{5,1},{6,2},{7,3},{8,12},{9,13},{10,... | collective-permute-start | bytes 36872 | tf_op jit(solution)/shard_map/ppermute | solution.py:343
  13.0 9.9 %collective-permute-start.7 = (f32[160,512]{1,0:T(8,128)S(1)}, f32[160,512]{1,0:T(8,128)S(1)}, u32[]{:S(2)}, u32[]{:S(2)}) collective-permute-start(f32[160,512]{1,0:T(8,128)S(1)} %slice.23), channel_id=1, source_target_pairs={{0,16},{1,17},{2,18},{3,19},{4,20},{5,21},{6,22},{7,23},{8,24},{9,... | collective-permute-start | bytes 983048 | tf_op jit(solution)/shard_map/ppermute | solution.py:351
  19.0 21.9 %collective-permute-start.8 = (bf16[160,1536]{1,0:T(8,128)(2,1)S(1)}, bf16[160,1536]{1,0:T(8,128)(2,1)S(1)}, u32[]{:S(2)}, u32[]{:S(2)}) collective-permute-start(bf16[160,1536]{1,0:T(8,128)(2,1)S(1)} %select_convert_fusion.refs_0_), channel_id=1, source_target_pairs={{0,4},{1,5},{2,6},{3,7},{4,0},{5,1},{6,2},{7,3},{8,12},{9,13},{10,... | collective-permute-start | bytes 1474568 | tf_op jit(solution)/shard_map/ppermute | solution.py:343
  19.1 23.1 %collective-permute-start.6 = (bf16[160,1536]{1,0:T(8,128)(2,1)S(1)}, bf16[160,1536]{1,0:T(8,128)(2,1)S(1)}, u32[]{:S(2)}, u32[]{:S(2)}) collective-permute-start(bf16[160,1536]{1,0:T(8,128)(2,1)S(1)} %select_convert_fusion.refs_0_), channel_id=1, source_target_pairs={{0,8},{1,9},{2,10},{3,11},{4,12},{5,13},{6,14},{7,15},{8,0},{9,1},... | collective-permute-start | bytes 1474568 | tf_op jit(solution)/shard_map/ppermute | solution.py:343
  21.5 21.1 %collective-permute-start.10 = (bf16[160,1536]{1,0:T(8,128)(2,1)S(1)}, bf16[160,1536]{1,0:T(8,128)(2,1)}, u32[]{:S(2)}, u32[]{:S(2)}) collective-permute-start(bf16[160,1536]{1,0:T(8,128)(2,1)S(1)} %select_convert_fusion.refs_0_), channel_id=1, source_target_pairs={{0,2},{1,3},{2,0},{3,1},{4,6},{5,7},{6,4},{7,5},{8,10},{9,11},{10,... | collective-permute-start | bytes 1474568 | tf_op jit(solution)/shard_map/ppermute | solution.py:343
  42.2 11.4 %collective-permute-start.9 = (bf16[160,1536]{1,0:T(8,128)(2,1)S(1)}, bf16[160,1536]{1,0:T(8,128)(2,1)S(1)}, u32[]{:S(2)}, u32[]{:S(2)}) collective-permute-start(bf16[160,1536]{1,0:T(8,128)(2,1)S(1)} %shard_map.41), channel_id=1, source_target_pairs={{0,4},{1,5},{2,6},{3,7},{4,0},{5,1},{6,2},{7,3},{8,12},{9,13},{10,... | collective-permute-start | bytes 1474568 | tf_op jit(solution)/shard_map/ppermute | solution.py:343
  42.6 22.7 %collective-permute-start.15 = (bf16[160,1536]{1,0:T(8,128)(2,1)S(1)}, bf16[160,1536]{1,0:T(8,128)(2,1)S(1)}, u32[]{:S(2)}, u32[]{:S(2)}) collective-permute-start(bf16[160,1536]{1,0:T(8,128)(2,1)S(1)} %select_convert_fusion.refs_0_), channel_id=1, source_target_pairs={{0,1},{1,0},{2,3},{3,2},{4,5},{5,4},{6,7},{7,6},{8,9},{9,8},{10,11... | collective-permute-start | bytes 1474568 | tf_op jit(solution)/shard_map/ppermute | solution.py:343
  42.6 22.8 %collective-permute-start.16 = (bf16[160,1536]{1,0:T(8,128)(2,1)}, bf16[160,1536]{1,0:T(8,128)(2,1)S(1)}, u32[]{:S(2)}, u32[]{:S(2)}) collective-permute-start(bf16[160,1536]{1,0:T(8,128)(2,1)} %collective-permute-done.10.refs_1_.refs_2_), channel_id=1, source_target_pairs={{0,1},{1,0},{2,3},{3,2},{4,5},{5,4},{6,7},{7,6},{8,9},{9,8},{10,11... | collective-permute-start | bytes 1474568 | tf_op jit(solution)/shard_map/ppermute | solution.py:343
  53.6 14.5 %collective-permute-start.13 = (f32[160,512]{1,0:T(8,128)S(1)}, f32[160,512]{1,0:T(8,128)S(1)}, u32[]{:S(2)}, u32[]{:S(2)}) collective-permute-start(f32[160,512]{1,0:T(8,128)S(1)} %shard_map.43), channel_id=1, source_target_pairs={{0,4},{1,5},{2,6},{3,7},{4,0},{5,1},{6,2},{7,3},{8,12},{9,13},{10,... | collective-permute-start | bytes 983048 | tf_op jit(solution)/shard_map/ppermute | solution.py:343
  54.0 14.9 %collective-permute-start.14 = (f32[160,512]{1,0:T(8,128)S(1)}, f32[160,512]{1,0:T(8,128)}, u32[]{:S(2)}, u32[]{:S(2)}) collective-permute-start(f32[160,512]{1,0:T(8,128)S(1)} %shard_map.43), channel_id=1, source_target_pairs={{0,8},{1,9},{2,10},{3,11},{4,12},{5,13},{6,14},{7,15},{8,0},{9,1},... | collective-permute-start | bytes 983048 | tf_op jit(solution)/shard_map/ppermute | solution.py:343
  60.5 8.9 %collective-permute-start.12 = (bf16[160,1536]{1,0:T(8,128)(2,1)S(1)}, bf16[160,1536]{1,0:T(8,128)(2,1)S(1)}, u32[]{:S(2)}, u32[]{:S(2)}) collective-permute-start(bf16[160,1536]{1,0:T(8,128)(2,1)S(1)} %select_select_fusion.refs_1_.refs_0_.refs_4_), channel_id=1, source_target_pairs={{0,2},{1,3},{2,0},{3,1},{4,6},{5,7},{6,4},{7,5},{8,10},{9,11},{10,... | collective-permute-start | bytes 1474568 | tf_op jit(solution)/shard_map/ppermute | solution.py:343
  74.1 11.0 %collective-permute-start.18 = (f32[168,512]{1,0:T(8,128)S(1)}, f32[168,512]{1,0:T(8,128)S(1)}, u32[]{:S(2)}, u32[]{:S(2)}) collective-permute-start(f32[168,512]{1,0:T(8,128)S(1)} %concatenate.6.refs_8_), channel_id=1, source_target_pairs={{0,16},{16,0},{1,17},{17,1},{2,18},{18,2},{3,19},{19,3},{4,20},{20... | collective-permute-start | bytes 1032200 | tf_op jit(solution)/shard_map/ppermute | solution.py:346
  75.4 11.7 %collective-permute-start.19 = (f32[160,512]{1,0:T(8,128)}, f32[160,512]{1,0:T(8,128)S(1)}, u32[]{:S(2)}, u32[]{:S(2)}) collective-permute-start(f32[160,512]{1,0:T(8,128)} %collective-permute-done.14.refs_2_), channel_id=1, source_target_pairs={{0,4},{1,5},{2,6},{3,7},{4,0},{5,1},{6,2},{7,3},{8,12},{9,13},{10,... | collective-permute-start | bytes 983048 | tf_op jit(solution)/shard_map/ppermute | solution.py:343
  79.7 18.6 %collective-permute-start.20 = (f32[320,512]{1,0:T(8,128)}, f32[320,512]{1,0:T(8,128)S(1)}, u32[]{:S(2)}, u32[]{:S(2)}) collective-permute-start(f32[320,512]{1,0:T(8,128)} %get-tuple-element.19.refs_1_), channel_id=1, source_target_pairs={{0,16},{16,0},{1,17},{17,1},{2,18},{18,2},{3,19},{19,3},{4,20},{20... | collective-permute-start | bytes 1966088 | tf_op jit(solution)/shard_map/ppermute | solution.py:346
  89.1 8.5 %collective-permute-start.24 = (f32[160,512]{1,0:T(8,128)}, f32[160,512]{1,0:T(8,128)}, u32[]{:S(2)}, u32[]{:S(2)}) collective-permute-start(f32[160,512]{1,0:T(8,128)} %shard_map.49.refs_5_.refs_1_), channel_id=1, source_target_pairs={{0,2},{1,3},{2,0},{3,1},{4,6},{5,7},{6,4},{7,5},{8,10},{9,11},{10,... | collective-permute-start | bytes 983048 | tf_op jit(solution)/shard_map/ppermute | solution.py:343
  90.0 9.5 %collective-permute-start.23 = (f32[160,512]{1,0:T(8,128)}, f32[160,512]{1,0:T(8,128)}, u32[]{:S(2)}, u32[]{:S(2)}) collective-permute-start(f32[160,512]{1,0:T(8,128)} %shard_map.49.refs_5_.refs_1_), channel_id=1, source_target_pairs={{0,1},{1,0},{2,3},{3,2},{4,5},{5,4},{6,7},{7,6},{8,9},{9,8},{10,11... | collective-permute-start | bytes 983048 | tf_op jit(solution)/shard_map/ppermute | solution.py:343
  98.3 20.4 %collective-permute-start.21 = (f32[320,640]{1,0:T(8,128)S(1)}, f32[320,640]{1,0:T(8,128)S(1)}, u32[]{:S(2)}, u32[]{:S(2)}) collective-permute-start(f32[320,640]{1,0:T(8,128)S(1)} %shard_map.51), channel_id=1, source_target_pairs={{0,16},{16,0},{1,17},{17,1},{2,18},{18,2},{3,19},{19,3},{4,20},{20... | collective-permute-start | bytes 2457608 | tf_op jit(solution)/shard_map/ppermute | solution.py:346
  111.6 18.1 %collective-permute-start.30 = (f32[320,512]{1,0:T(8,128)S(1)}, f32[320,512]{1,0:T(8,128)S(1)}, u32[]{:S(2)}, u32[]{:S(2)}) collective-permute-start(f32[320,512]{1,0:T(8,128)S(1)} %pad_maximum_fusion.refs_2_.refs_4_), channel_id=1, source_target_pairs={{0,2},{1,3},{2,0},{3,1},{4,6},{5,7},{6,4},{7,5},{8,10},{9,11},{10,... | collective-permute-start | bytes 1966088 | tf_op jit(solution)/shard_map/ppermute | solution.py:343
  112.8 26.8 %collective-permute-start.29 = (f32[320,512]{1,0:T(8,128)S(1)}, f32[320,512]{1,0:T(8,128)S(1)}, u32[]{:S(2)}, u32[]{:S(2)}) collective-permute-start(f32[320,512]{1,0:T(8,128)S(1)} %pad_maximum_fusion.refs_2_.refs_4_), channel_id=1, source_target_pairs={{0,1},{1,0},{2,3},{3,2},{4,5},{5,4},{6,7},{7,6},{8,9},{9,8},{10,11... | collective-permute-start | bytes 1966088 | tf_op jit(solution)/shard_map/ppermute | solution.py:343
  121.3 18.3 %collective-permute-start.26 = (f32[160,320]{1,0:T(8,128)S(1)}, f32[160,320]{1,0:T(8,128)S(1)}, u32[]{:S(2)}, u32[]{:S(2)}) collective-permute-start(f32[160,320]{1,0:T(8,128)S(1)} %get-tuple-element.20.refs_1_.refs_2_), channel_id=1, source_target_pairs={{0,1},{1,0},{2,3},{3,2},{4,5},{5,4},{6,7},{7,6},{8,9},{9,8},{10,11... | collective-permute-start | bytes 614408 | tf_op jit(solution)/shard_map/ppermute | solution.py:343
  121.9 12.4 %collective-permute-start.22 = (f32[160,512]{1,0:T(8,128)S(1)}, f32[160,512]{1,0:T(8,128)S(1)}, u32[]{:S(2)}, u32[]{:S(2)}) collective-permute-start(f32[160,512]{1,0:T(8,128)S(1)} %shard_map.53), channel_id=1, source_target_pairs={{0,16},{16,0},{1,17},{17,1},{2,18},{18,2},{3,19},{19,3},{4,20},{20... | collective-permute-start | bytes 983048 | tf_op jit(solution)/shard_map/ppermute | solution.py:346
  122.6 17.1 %collective-permute-start.27 = (f32[160,320]{1,0:T(8,128)S(1)}, f32[160,320]{1,0:T(8,128)S(1)}, u32[]{:S(2)}, u32[]{:S(2)}) collective-permute-start(f32[160,320]{1,0:T(8,128)S(1)} %get-tuple-element.33), channel_id=1, source_target_pairs={{0,2},{1,3},{2,0},{3,1},{4,6},{5,7},{6,4},{7,5},{8,10},{9,11},{10,... | collective-permute-start | bytes 614408 | tf_op jit(solution)/shard_map/ppermute | solution.py:343
  129.7 12.3 %collective-permute-start.31 = (f32[320,512]{1,0:T(8,128)S(1)}, f32[320,512]{1,0:T(8,128)S(1)}, u32[]{:S(2)}, u32[]{:S(2)}) collective-permute-start(f32[320,512]{1,0:T(8,128)S(1)} %shard_map.61.refs_6_), channel_id=1, source_target_pairs={{0,1},{1,0},{2,3},{3,2},{4,5},{5,4},{6,7},{7,6},{8,9},{9,8},{10,11... | collective-permute-start | bytes 1966088 | tf_op jit(solution)/shard_map/ppermute | solution.py:343
  134.3 7.7 %collective-permute-start.28 = (f32[160,320]{1,0:T(8,128)S(1)}, f32[160,320]{1,0:T(8,128)S(1)}, u32[]{:S(2)}, u32[]{:S(2)}) collective-permute-start(f32[160,320]{1,0:T(8,128)S(1)} %get-tuple-element.34), channel_id=1, source_target_pairs={{0,3},{1,2},{2,1},{3,0},{4,7},{5,6},{6,5},{7,4},{8,11},{9,10},{10,... | collective-permute-start | bytes 614408 | tf_op jit(solution)/shard_map/ppermute | solution.py:343
  (43 other events, 228.5 us)
where the time goes:
time: 146 us; the launch traced here: 145 us
  waiting for transfers between devices  51.6 us (35%)
  Pallas kernels  44.6 us (31%)
  starting transfers between devices  31.4 us (22%)
  other arithmetic  9.23 us (6%)
  local copies, waits for them, and re-layouts  5.41 us (4%)
  between operations  3.24 us (2%)
    ppermute x27, waiting for transfers between devices, rows_xor(): return lax.ppermute(x, 'rows', [(r, r ^ bits) for r in range(n_rows)])  45.6 us
    ppermute x27, starting transfers between devices, rows_xor(): return lax.ppermute(x, 'rows', [(r, r ^ bits) for r in range(n_rows)])  23.8 us
    pallas_call x4, Pallas kernels, factor_step(): pl.pallas_call(kernel, out_shape=out_shape, in_specs=[SMEM] + [VMEM] * n_...  23 us
    pallas_call x3, Pallas kernels, head_products(): pl.pallas_call(functools.partial(head_kernel, len(left), sizes), out_shap...  8.07 us
    ppermute x4, waiting for transfers between devices, snp_xor(): return lax.ppermute(x, 'snp', [(s, s ^ bits) for s in range(n_snp)])  5.28 us
    pallas_call x2, Pallas kernels, gram_products(): pl.pallas_call(kernel, out_shape=out_shape, in_specs=[VMEM] * (GROUP + le...  5.2 us
    pallas_call x1, Pallas kernels, solve(): pl.pallas_call(functools.partial(solve_kernel, len(inverses)), out_shape=...  4.39 us
    ppermute x4, starting transfers between devices, snp_xor(): return lax.ppermute(x, 'snp', [(s, s ^ bits) for s in range(n_snp)])  4.11 us
  transfers between devices with their start and end apart: 32, of which 14 were waited for; matrix products, arithmetic and copies ran while one was open for 6% of the time, Pallas kernels for 27%

commit v1 on v0

--- a/solution.py
+++ b/solution.py
@@ -165,12 +165,17 @@
     )(place, *squares, *waits)
 
 
-def solve_kernel(blocks, columns, *refs):
+def solve_kernel(blocks, n_lead, rel, scale, *refs):
+    lead, refs = refs[:n_lead], refs[n_lead:]
     inverses, below = refs[:blocks], refs[blocks : 2 * blocks - 1]
     panel, weights = refs[-2:]
     found = []
     for k in range(blocks):
-        total = columns[:, k * BLOCK : (k + 1) * BLOCK]
+        across = slice(k * BLOCK, (k + 1) * BLOCK)
+        total = lead[0][:, across]
+        for x in lead[1:]:
+            total = total + x[:, across]
+        total = rel[:, across] + total * scale[0:1, :]
         for j in range(k):
             start = (k - j - 1) * BLOCK
             total = total - precise(found[j], below[j][start : start + BLOCK, :], 1)
@@ -185,16 +190,16 @@
         weights[:, k * BLOCK : (k + 1) * BLOCK] = found[k]
 
 
-def solve(columns, inverses, below):
-    own = columns.shape[0]
-    return pl.pallas_call(
-        functools.partial(solve_kernel, len(inverses)),
+def solve(rel, scale, lead, inverses, below):
+    own = rel.shape[0]
+    return pl.pallas_call(
+        functools.partial(solve_kernel, len(inverses), len(lead)),
         out_shape=[f32(own, PANEL), f32(own, PANEL)],
-        in_specs=[VMEM] * (2 * len(inverses)),
+        in_specs=[VMEM] * (1 + len(lead) + 2 * len(inverses)),
         out_specs=[VMEM, VMEM],
-        compiler_params=room(columns, columns, columns, *inverses, *below),
+        compiler_params=room(rel, rel, rel, *lead, *inverses, *below),
         cost_estimate=cost(4 * own * PANEL * PANEL),
-    )(columns, *inverses, *below)
+    )(rel, scale, *lead, *inverses, *below)
 
 
 def head_kernel(n_left, sizes, place, *refs):
@@ -207,6 +212,72 @@
         for n in range(count):
             out[n * own : (n + 1) * own, :] = times(left[at][...], order[:PANEL, :])
             at += 1
+
+
+def message_kernel(place, scale, first, *refs):
+    head, out, order = refs[:GROUP], refs[-2], refs[-1]
+    own = first.shape[0]
+    in_order(place, head, order)
+    out[:own, :] = times(first[...], order[:PANEL, :])
+    out[own:, :] = jnp.full((SUB, PANEL), scale[0], jnp.float32)
+
+
+def message(place, scale, first, head):
+    own, depth = first.shape
+    return pl.pallas_call(
+        message_kernel,
+        out_shape=f32(own + SUB, PANEL),
+        in_specs=[SMEM, SMEM] + [VMEM] * (1 + GROUP),
+        out_specs=VMEM,
+        scratch_shapes=[pltpu.VMEM((GROUP * own, depth), first.dtype)],
+        compiler_params=room(first, *head, *head, f32(own, PANEL)),
+        cost_estimate=cost(2 * own * PANEL * depth),
+    )(place, scale, first, *head)
+
+
+def total_kernel(*refs):
+    parts, (rel, total, inverse) = refs[:-3], refs[-3:]
+    own = total.shape[0]
+    value = parts[0][...]
+    for x in parts[1:]:
+        value = value + x[...]
+    scale = 1.0 / value[own : own + 1, :]
+    total[...] = rel[...] + value[:own, :] * scale
+    inverse[...] = jnp.broadcast_to(scale[:, :BLOCK], (SUB, BLOCK))
+
+
+def total_rows(parts, rel):
+    return pl.pallas_call(
+        total_kernel,
+        out_shape=[f32(*rel.shape), f32(SUB, BLOCK)],
+        in_specs=[VMEM] * (len(parts) + 1),
+        out_specs=[VMEM] * 2,
+        compiler_params=room(*parts, rel, rel),
+        cost_estimate=cost(1_000_000),
+    )(*parts, rel)
+
+
+def side_kernel(n_parts, n_rel, scale, *refs):
+    parts, rel, out = refs[:n_parts], refs[n_parts : n_parts + n_rel], refs[-1]
+    own = rel[0].shape[0]
+    factor = scale[0:1, 0:1]
+    for n in range(n_rel):
+        cut = slice(n * own, (n + 1) * own)
+        value = parts[0][cut, :]
+        for x in parts[1:]:
+            value = value + x[cut, :]
+        out[cut, :] = rel[n][...] + value * factor
+
+
+def side_rows(scale, parts, rel, waits):
+    return pl.pallas_call(
+        functools.partial(side_kernel, len(parts), len(rel)),
+        out_shape=f32(*parts[0].shape),
+        in_specs=[VMEM] * (1 + len(parts) + len(rel)) + [ANYWHERE] * len(waits),
+        out_specs=VMEM,
+        compiler_params=room(*parts, *rel, parts[0]),
+        cost_estimate=cost(1_000_000),
+    )(scale, *parts, *rel, *waits)
 
 
 def head_products(place, groups, head, waits):
@@ -287,7 +358,7 @@
             cut = slice(n * own, (n + 1) * own)
             here = (place[0] == m) & (place[1] == n)
             value = rel[:, at : at + own] - product[:, cut]
-            value = value + all_pieces[m * own : (m + 1) * own, cut] * scale[0]
+            value = value + all_pieces[m * own : (m + 1) * own, cut] * scale[0:1, 0:1]
             out[:, at : at + own] = value + ridge * jnp.where(here, 1.0, 0.0)
 
 
@@ -297,7 +368,7 @@
     return pl.pallas_call(
         functools.partial(update_kernel, own, part),
         out_shape=f32(own, width),
-        in_specs=[SMEM, SMEM] + [VMEM] * (2 + 2 * GROUP),
+        in_specs=[SMEM] + [VMEM] * (3 + 2 * GROUP),
         out_specs=VMEM,
         scratch_shapes=[
             pltpu.VMEM((GROUP * own, part * own), jnp.float32),
@@ -425,16 +496,13 @@
         head = [first, rows_xor(first, 1)]
         head.append(after(rows_xor(first, 2), *rel_line[1 : far + 1], *leaving))
         head.append(rows_xor(head[2], 1))
-        (rows,) = head_products(place, [[first]], head, [])
-        rows = jnp.concatenate(
-            [rows, jnp.broadcast_to(scale_part.reshape(1, 1), (SUB, PANEL))], axis=0
-        )
-        total = snp_sum(rows)
-        inverse = 1.0 / total[own, 0]
-        total = total[:own] * inverse + select_order(rel_line, z)[0]
+        rows = message(place, scale_part.reshape(1), first, head)
+        rows_got = [snp_xor(rows, bits) for bits in range(1, n_snp)]
         sides = head_products(place, groups, head, [rows])
+        total, scale = total_rows([rows] + rows_got, select_order(rel_line, z)[0])
+        sides = [sides[0]] + [after(x, total) for x in sides[1:]]
+        side_got = [snp_xor(sides[bits], bits) for bits in range(1, n_snp)]
         total = after(total, *sides[1:])
-        side_got = [snp_xor(sides[bits], bits) for bits in range(1, n_snp)]
 
         (lead,) = head_products(place, [[centered]], head, [total])
         diagonal = [total, rows_xor(total, 1)]
@@ -449,20 +517,13 @@
 
         inv, column, square = factor_step(place, diagonal, PANEL, side_got)
         inverses, below = [inv], [column]
-        side = sides[0]
-        for got in side_got:
-            side = side + after(got, inverses[0])
         rel_side = select_order(rel_line, z ^ (col * part))[:part]
-        side = jnp.concatenate(
-            [
-                rel_side[j] + side[j * own : (j + 1) * own] * inverse
-                for j in range(part)
-            ],
-            axis=0,
-        )
+        side = side_rows(scale, [sides[0]] + side_got, rel_side, [inverses[0]])
         sides = [side, rows_xor(side, 1), rows_xor(side, 2)]
 
-        waits = [[], [side], [pieces[1]], []]
+        lead = after(lead, pieces[1])
+        leads = [lead] + [snp_xor(lead, bits) for bits in range(1, n_snp)]
+        waits = [[], [side], [pieces[1], sides[1]], leads[1:] + [moved[2]]]
         for k in range(1, PANEL // BLOCK):
             inv, *more = factor_step(place, [square], PANEL - k * BLOCK, waits[k])
             inverses.append(inv)
@@ -473,11 +534,8 @@
         sides[2] = after(sides[2], inverses[2])
         sides.append(rows_xor(sides[2], 1))
 
-        own_columns = rel_own + snp_sum(after(lead, pieces[1])) * inverse
-        panel, weights = solve(own_columns, inverses, below)
-        updated = final_update(
-            place, inverse.reshape(1), relationship, weights, moved, sides
-        )
+        panel, weights = solve(rel_own, scale, leads, inverses, below)
+        updated = final_update(place, scale, relationship, weights, moved, sides)
         return updated, panel
 
     return per_device

time: 146 us -> 141 us (0.966)
  waiting for transfers between devices: 51.6 us -> 57.8 us
  local copies, waits for them, and re-layouts: 5.41 us -> 0.15 us
  other arithmetic: 9.23 us -> 6.4 us
  Pallas kernels: 44.6 us -> 41.9 us
    add x5 -> x0, other arithmetic: 4.04 us -> none  [the longest x1 1.98 us: per_device(): total = total[:own] * inverse + select_order(rel_line, z)[0]]
    unnamed x71 -> x41, local copies, waits for them, and re-layouts: 4.06 us -> 0.11 us
    ppermute x4, waiting for transfers between devices: 5.28 us -> 8.92 us  [snp_xor(): return lax.ppermute(x, 'snp', [(s, s ^ bits) for s in range(n_snp)])]
    ppermute x27, waiting for transfers between devices: 45.6 us -> 48.7 us  [rows_xor(): return lax.ppermute(x, 'rows', [(r, r ^ bits) for r in range(n_rows)])]
    pallas_call x1 -> x4, Pallas kernels: 4.39 us -> 7.28 us  [the longest x1 4.4 us: solve(): pl.pallas_call(functools.partial(solve_kernel, len(inverses), len(lead)),...]
    pallas_call x3 -> x2, Pallas kernels: 8.07 us -> 5.47 us  [head_products(): pl.pallas_call(functools.partial(head_kernel, len(left), sizes), out_shap...]
    pallas_call x2, Pallas kernels: 5.2 us -> 2.79 us  [gram_products(): pl.pallas_call(kernel, out_shape=out_shape, in_specs=[VMEM] * (GROUP + le...]
    ppermute x4, starting transfers between devices: 4.11 us -> 6.46 us  [snp_xor(): return lax.ppermute(x, 'snp', [(s, s ^ bits) for s in range(n_snp)])]
  transfers between devices with their start and end apart: 32 -> 32, of which waited for: 14 -> 15; matrix products, arithmetic and copies ran while one was open for 6% -> 3% of each run, Pallas kernels for 27% -> 27%
where the time goes in v1:
time: 141 us
  waiting for transfers between devices  57.8 us (41%)
  Pallas kernels  41.9 us (30%)
  starting transfers between devices  32.5 us (23%)
  other arithmetic  6.4 us (5%)
  between operations  2.37 us (2%)
    ppermute x27, waiting for transfers between devices, rows_xor(): return lax.ppermute(x, 'rows', [(r, r ^ bits) for r in range(n_rows)])  48.7 us
    ppermute x27, starting transfers between devices, rows_xor(): return lax.ppermute(x, 'rows', [(r, r ^ bits) for r in range(n_rows)])  22.6 us
    pallas_call x4, Pallas kernels, factor_step(): pl.pallas_call(kernel, out_shape=out_shape, in_specs=[SMEM] + [VMEM] * n_...  22.4 us
    ppermute x4, waiting for transfers between devices, snp_xor(): return lax.ppermute(x, 'snp', [(s, s ^ bits) for s in range(n_snp)])  8.92 us
    ppermute x4, starting transfers between devices, snp_xor(): return lax.ppermute(x, 'snp', [(s, s ^ bits) for s in range(n_snp)])  6.46 us
    pallas_call x2, Pallas kernels, head_products(): pl.pallas_call(functools.partial(head_kernel, len(left), sizes), out_shap...  5.47 us
    pallas_call x1, Pallas kernels, solve(): pl.pallas_call(functools.partial(solve_kernel, len(inverses), len(lead)),...  4.4 us
    select_n x3, other arithmetic, select_order(): jnp.where(swap, blocks[k ^ bit], blocks[k])  3.87 us
  transfers between devices with their start and end apart: 32, of which 15 were waited for; matrix products, arithmetic and copies ran while one was open for 3% of the time, Pallas kernels for 27%

profile of v1, /device:TPU:0, one launch (start us, length us, event | category | flops | bytes accessed | tf_op | source)
XLA Modules:
  0.0 141.2 jit_solution(4079715938394439488)
XLA Ops:
  2.2 3.0 %collective-permute-start.1 = (f32[2,1536]{1,0:T(2,128)S(1)}, f32[2,1536]{1,0:T(2,128)S(1)}, u32[]{:S(2)}, u32[]{:S(2)}) collective-permute-start(f32[2,1536]{1,0:T(2,128)S(1)} %pad_maximum_fusion), channel_id=1, source_target_pairs={{0,2},{1,3},{2,0},{3,1},{4,6},{5,7},{6,4},{7,5},{8,10},{9,11},{10,... | collective-permute-start | bytes 36872 | tf_op jit(solution)/shard_map/ppermute | solution.py:414
  8.4 3.7 %collective-permute-start.5 = (f32[2,1536]{1,0:T(2,128)S(1)}, f32[2,1536]{1,0:T(2,128)S(1)}, u32[]{:S(2)}, u32[]{:S(2)}) collective-permute-start(f32[2,1536]{1,0:T(2,128)S(1)} %add_add_fusion.1), channel_id=1, source_target_pairs={{0,12},{1,13},{2,14},{3,15},{4,8},{5,9},{6,10},{7,11},{8,4},{9,5},... | collective-permute-start | bytes 36872 | tf_op jit(solution)/shard_map/ppermute | solution.py:414
  12.9 3.4 %collective-permute-start.7 = (f32[160,512]{1,0:T(8,128)S(1)}, f32[160,512]{1,0:T(8,128)S(1)}, u32[]{:S(2)}, u32[]{:S(2)}) collective-permute-start(f32[160,512]{1,0:T(8,128)S(1)} %slice.11), channel_id=1, source_target_pairs={{0,16},{1,17},{2,18},{3,19},{4,20},{5,21},{6,22},{7,23},{8,24},{9,... | collective-permute-start | bytes 983048 | tf_op jit(solution)/shard_map/ppermute | solution.py:422
  18.5 2.9 %collective-permute-start.6 = (bf16[160,1536]{1,0:T(8,128)(2,1)S(1)}, bf16[160,1536]{1,0:T(8,128)(2,1)S(1)}, u32[]{:S(2)}, u32[]{:S(2)}) collective-permute-start(bf16[160,1536]{1,0:T(8,128)(2,1)S(1)} %select_convert_fusion.refs_0_), channel_id=1, source_target_pairs={{0,8},{1,9},{2,10},{3,11},{4,12},{5,13},{6,14},{7,15},{8,0},{9,1},... | collective-permute-start | bytes 1474568 | tf_op jit(solution)/shard_map/ppermute | solution.py:414
  22.4 16.8 %collective-permute-done.8.refs_2_ = bf16[160,1536]{1,0:T(8,128)(2,1)S(1)} collective-permute-done((bf16[160,1536]{1,0:T(8,128)(2,1)S(1)}, bf16[160,1536]{1,0:T(8,128)(2,1)S(1)}, u32[]{:S(2)}, u32[]{:S(2)}) %collective-permute-start.8) | collective-permute-done | bytes 491552 | tf_op jit(solution)/shard_map/ppermute | solution.py:414
  39.2 2.4 %collective-permute-done.6.refs_0_ = bf16[160,1536]{1,0:T(8,128)(2,1)S(1)} collective-permute-done((bf16[160,1536]{1,0:T(8,128)(2,1)S(1)}, bf16[160,1536]{1,0:T(8,128)(2,1)S(1)}, u32[]{:S(2)}, u32[]{:S(2)}) %collective-permute-start.6) | collective-permute-done | bytes 491552 | tf_op jit(solution)/shard_map/ppermute | solution.py:414
  42.5 11.3 %collective-permute-done.9.refs_0_ = bf16[160,1536]{1,0:T(8,128)(2,1)S(1)} collective-permute-done((bf16[160,1536]{1,0:T(8,128)(2,1)S(1)}, bf16[160,1536]{1,0:T(8,128)(2,1)S(1)}, u32[]{:S(2)}, u32[]{:S(2)}) %collective-permute-start.9) | collective-permute-done | bytes 491552 | tf_op jit(solution)/shard_map/ppermute | solution.py:414
  53.7 2.4 %collective-permute-start.13 = (f32[160,512]{1,0:T(8,128)S(1)}, f32[160,512]{1,0:T(8,128)S(1)}, u32[]{:S(2)}, u32[]{:S(2)}) collective-permute-start(f32[160,512]{1,0:T(8,128)S(1)} %shard_map.43), channel_id=1, source_target_pairs={{0,4},{1,5},{2,6},{3,7},{4,0},{5,1},{6,2},{7,3},{8,12},{9,13},{10,... | collective-permute-start | bytes 983048 | tf_op jit(solution)/shard_map/ppermute | solution.py:414
  62.3 2.7 %collective-permute-done.14.refs_2_ = f32[160,512]{1,0:T(8,128)} collective-permute-done((f32[160,512]{1,0:T(8,128)S(1)}, f32[160,512]{1,0:T(8,128)}, u32[]{:S(2)}, u32[]{:S(2)}) %collective-permute-start.14) | collective-permute-done | bytes 327712 | tf_op jit(solution)/shard_map/ppermute | solution.py:414
  68.5 2.6 %shard_map.47.refs_0_.refs_8_ = f32[168,512]{1,0:T(8,128)S(1)} custom-call(s32[2]{0:T(128)S(1)} %pad_add_fusion.place.refs_0_, f32[1]{0:T(128)} %bitcast.2.scale, bf16[160,1536]{1,0:T(8,128)(2,1)S(1)} %select_select_fusion.refs_1_.first.refs_0_.refs_4_, bf16[160,1536]{1,0:T(8,128)(2,1)S(1)} %select_select_fusion.refs_1_.first.refs_0_.refs_4_, ...), custom_call_target="tpu_custom_call" | custom-call | flops 251658240 | bytes 131072 | tf_op jit(solution)/shard_map/pallas_call | solution.py:227
  72.9 4.0 %collective-permute-done.19 = f32[160,512]{1,0:T(8,128)} collective-permute-done((f32[160,512]{1,0:T(8,128)}, f32[160,512]{1,0:T(8,128)}, u32[]{:S(2)}, u32[]{:S(2)}) %collective-permute-start.19) | collective-permute-done | bytes 327712 | tf_op jit(solution)/shard_map/ppermute | solution.py:414
  78.2 3.5 %shard_map.49 = (f32[320,512]{1,0:T(8,128)S(1)}, f32[320,512]{1,0:T(8,128)S(1)}) custom-call(s32[2]{0:T(128)S(1)} %pad_add_fusion.place.refs_0_, bf16[160,1536]{1,0:T(8,128)(2,1)S(1)} %copy-done.1, bf16[160,1536]{1,0:T(8,128)(2,1)S(1)} %copy-done, bf16[160,1536]{1,0:T(8,128)(2,1)S(1)} %copy-done.5, bf16[160,1536]{1,0:T(8,128)(2,1)S(1)} %copy-done.3, ...), custom_call_target="tpu_custom_call" | custom-call | flops 1006632960 | bytes 131072 | tf_op jit(solution)/shard_map/pallas_call | solution.py:287
  85.2 2.0 %shard_map.52.refs_0_.refs_1_ = f32[160,512]{1,0:T(8,128)S(1)} custom-call(s32[2]{0:T(128)S(1)} %pad_add_fusion.place.refs_0_, bf16[160,1536]{1,0:T(8,128)(2,1)S(1)} %select_convert_fusion.refs_0_, bf16[160,1536]{1,0:T(8,128)(2,1)S(1)} %select_select_fusion.refs_1_.first.refs_0_.refs_4_, bf16[160,1536]{1,0:T(8,128)(2,1)} %collective-permute-done.11.refs_1_.refs_5_.refs_2_, ...), custom_call_target="tpu_custom_call" | custom-call | flops 251658240 | bytes 131072 | tf_op jit(solution)/shard_map/pallas_call | solution.py:287
  87.1 5.4 %collective-permute-done.24.refs_0_ = f32[160,512]{1,0:T(8,128)S(1)} collective-permute-done((f32[160,512]{1,0:T(8,128)S(1)}, f32[160,512]{1,0:T(8,128)S(1)}, u32[]{:S(2)}, u32[]{:S(2)}) %collective-permute-start.24) | collective-permute-done | bytes 327712 | tf_op jit(solution)/shard_map/ppermute | solution.py:414
  92.5 5.7 %collective-permute-done.20.refs_1_.refs_5_ = f32[320,512]{1,0:T(8,128)S(1)} collective-permute-done((f32[320,512]{1,0:T(8,128)S(1)}, f32[320,512]{1,0:T(8,128)S(1)}, u32[]{:S(2)}, u32[]{:S(2)}) %collective-permute-start.20) | collective-permute-done | bytes 655392 | tf_op jit(solution)/shard_map/ppermute | solution.py:417
  99.8 6.2 %shard_map.57 = (f32[128,128]{1,0:T(8,128)S(1)}, f32[384,128]{1,0:T(8,128)S(1)}, f32[384,384]{1,0:T(8,128)S(1)}) custom-call(s32[2]{0:T(128)S(1)} %pad_add_fusion.place.refs_0_, f32[160,512]{1,0:T(8,128)S(1)} %shard_map.51.refs_5_.refs_1_, f32[160,512]{1,0:T(8,128)S(1)} %collective-permute-done.23.refs_2_, f32[160,512]{1,0:T(8,128)S(1)} %shard_map.56.refs_3_, ...), custom_call_target="tpu_custom_call" | custom-call | flops 6000000000 | bytes 131072 | tf_op jit(solution)/shard_map/pallas_call | solution.py:157
  106.3 1.7 %collective-permute-start.30 = (f32[320,512]{1,0:T(8,128)S(1)}, f32[320,512]{1,0:T(8,128)S(1)}, u32[]{:S(2)}, u32[]{:S(2)}) collective-permute-start(f32[320,512]{1,0:T(8,128)S(1)} %shard_map.58.refs_2_.refs_4_), channel_id=1, source_target_pairs={{0,2},{1,3},{2,0},{3,1},{4,6},{5,7},{6,4},{7,5},{8,10},{9,11},{10,... | collective-permute-start | bytes 1966088 | tf_op jit(solution)/shard_map/ppermute | solution.py:414
  108.0 5.9 %shard_map.59 = (f32[128,128]{1,0:T(8,128)S(1)}, f32[256,128]{1,0:T(8,128)S(1)}, f32[256,256]{1,0:T(8,128)S(1)}) custom-call(s32[2]{0:T(128)S(1)} %pad_add_fusion.place.refs_0_, f32[384,384]{1,0:T(8,128)S(1)} %get-tuple-element.26.refs_1_, f32[320,512]{1,0:T(8,128)S(1)} %shard_map.58.refs_2_.refs_4_), custom_call_target="tpu_custom_call" | custom-call | flops 6000000000 | bytes 131072 | tf_op jit(solution)/shard_map/pallas_call | solution.py:157
  113.9 3.3 %collective-permute-done.21.refs_6_ = f32[320,640]{1,0:T(8,128)S(1)} collective-permute-done((f32[320,640]{1,0:T(8,128)S(1)}, f32[320,640]{1,0:T(8,128)S(1)}, u32[]{:S(2)}, u32[]{:S(2)}) %collective-permute-start.21) | collective-permute-done | bytes 819232 | tf_op jit(solution)/shard_map/ppermute | solution.py:417
  118.7 1.9 %collective-permute-start.27 = (f32[160,320]{1,0:T(8,128)S(1)}, f32[160,320]{1,0:T(8,128)S(1)}, u32[]{:S(2)}, u32[]{:S(2)}) collective-permute-start(f32[160,320]{1,0:T(8,128)S(1)} %get-tuple-element.32), channel_id=1, source_target_pairs={{0,2},{1,3},{2,0},{3,1},{4,6},{5,7},{6,4},{7,5},{8,10},{9,11},{10,... | collective-permute-start | bytes 614408 | tf_op jit(solution)/shard_map/ppermute | solution.py:414
  122.1 5.7 %shard_map.60 = (f32[128,128]{1,0:T(8,128)S(1)}, f32[128,128]{1,0:T(8,128)S(1)}, f32[128,128]{1,0:T(8,128)S(1)}) custom-call(s32[2]{0:T(128)S(1)} %pad_add_fusion.place.refs_0_, f32[256,256]{1,0:T(8,128)S(1)} %get-tuple-element.29.refs_1_, f32[160,320]{1,0:T(8,128)S(1)} %get-tuple-element.24.refs_1_.refs_2_, ...), custom_call_target="tpu_custom_call" | custom-call | flops 6000000000 | bytes 131072 | tf_op jit(solution)/shard_map/pallas_call | solution.py:157
  128.7 4.5 %shard_map.61.refs_5_ = f32[128,128]{1,0:T(8,128)S(1)} custom-call(s32[2]{0:T(128)S(1)} %pad_add_fusion.place.refs_0_, f32[128,128]{1,0:T(8,128)S(1)} %get-tuple-element.31.refs_1_, f32[160,512]{1,0:T(8,128)S(1)} %collective-permute-done.22.refs_2_.refs_1_, f32[160,320]{1,0:T(8,128)S(1)} %collective-permute-done.27.refs_3_.refs_2_), custom_call_target="tpu_custom_call" | custom-call | flops 6000000000 | bytes 131072 | tf_op jit(solution)/shard_map/pallas_call | solution.py:157
  133.3 4.4 %shard_map.62 = (f32[160,512]{1,0:T(8,128)}, f32[160,512]{1,0:T(8,128)S(1)}) custom-call(f32[160,512]{1,0:T(8,128)S(1)} %select_add_fusion.refs_1_.rel, f32[8,128]{1,0:T(8,128)S(1)} %get-tuple-element.21.scale, f32[160,512]{1,0:T(8,128)S(1)} %shard_map.55.refs_0_, f32[160,512]{1,0:T(8,128)S(1)} %collective-permute-done.22.refs_2_.refs_1_, ...), custom_call_target="tpu_custom_call" | custom-call | flops 167772160 | bytes 131072 | tf_op jit(solution)/shard_map/pallas_call | solution.py:195
  137.7 3.5 %shard_map.64 = f32[160,1280]{1,0:T(8,128)} custom-call(s32[2]{0:T(128)S(1)} %pad_add_fusion.place.refs_0_, f32[8,128]{1,0:T(8,128)S(1)} %get-tuple-element.21.scale, f32[160,1280]{1,0:T(8,128)S(1)} %copy-done.11, f32[160,512]{1,0:T(8,128)S(1)} %get-tuple-element.36.weights, f32[160,320]{1,0:T(8,128)S(1)} %get-tuple-element.37.refs_0_, ...), custom_call_target="tpu_custom_call" | custom-call | flops 209715200 | bytes 131072 | tf_op jit(solution)/shard_map/pallas_call | solution.py:368
  (120 shorter events, 29.8 us)
Async XLA Ops:
  8.4 7.9 %collective-permute-start.5 = (f32[2,1536]{1,0:T(2,128)S(1)}, f32[2,1536]{1,0:T(2,128)S(1)}, u32[]{:S(2)}, u32[]{:S(2)}) collective-permute-start(f32[2,1536]{1,0:T(2,128)S(1)} %add_add_fusion.1), channel_id=1, source_target_pairs={{0,12},{1,13},{2,14},{3,15},{4,8},{5,9},{6,10},{7,11},{8,4},{9,5},... | collective-permute-start | bytes 36872 | tf_op jit(solution)/shard_map/ppermute | solution.py:414
  12.9 9.4 %collective-permute-start.7 = (f32[160,512]{1,0:T(8,128)S(1)}, f32[160,512]{1,0:T(8,128)S(1)}, u32[]{:S(2)}, u32[]{:S(2)}) collective-permute-start(f32[160,512]{1,0:T(8,128)S(1)} %slice.11), channel_id=1, source_target_pairs={{0,16},{1,17},{2,18},{3,19},{4,20},{5,21},{6,22},{7,23},{8,24},{9,... | collective-permute-start | bytes 983048 | tf_op jit(solution)/shard_map/ppermute | solution.py:422
  17.5 21.8 %collective-permute-start.8 = (bf16[160,1536]{1,0:T(8,128)(2,1)S(1)}, bf16[160,1536]{1,0:T(8,128)(2,1)S(1)}, u32[]{:S(2)}, u32[]{:S(2)}) collective-permute-start(bf16[160,1536]{1,0:T(8,128)(2,1)S(1)} %select_convert_fusion.refs_0_), channel_id=1, source_target_pairs={{0,4},{1,5},{2,6},{3,7},{4,0},{5,1},{6,2},{7,3},{8,12},{9,13},{10,... | collective-permute-start | bytes 1474568 | tf_op jit(solution)/shard_map/ppermute | solution.py:414
  18.5 23.1 %collective-permute-start.6 = (bf16[160,1536]{1,0:T(8,128)(2,1)S(1)}, bf16[160,1536]{1,0:T(8,128)(2,1)S(1)}, u32[]{:S(2)}, u32[]{:S(2)}) collective-permute-start(bf16[160,1536]{1,0:T(8,128)(2,1)S(1)} %select_convert_fusion.refs_0_), channel_id=1, source_target_pairs={{0,8},{1,9},{2,10},{3,11},{4,12},{5,13},{6,14},{7,15},{8,0},{9,1},... | collective-permute-start | bytes 1474568 | tf_op jit(solution)/shard_map/ppermute | solution.py:414
  21.4 20.5 %collective-permute-start.10 = (bf16[160,1536]{1,0:T(8,128)(2,1)S(1)}, bf16[160,1536]{1,0:T(8,128)(2,1)S(1)}, u32[]{:S(2)}, u32[]{:S(2)}) collective-permute-start(bf16[160,1536]{1,0:T(8,128)(2,1)S(1)} %select_convert_fusion.refs_0_), channel_id=1, source_target_pairs={{0,2},{1,3},{2,0},{3,1},{4,6},{5,7},{6,4},{7,5},{8,10},{9,11},{10,... | collective-permute-start | bytes 1474568 | tf_op jit(solution)/shard_map/ppermute | solution.py:414
  41.6 12.1 %collective-permute-start.9 = (bf16[160,1536]{1,0:T(8,128)(2,1)S(1)}, bf16[160,1536]{1,0:T(8,128)(2,1)S(1)}, u32[]{:S(2)}, u32[]{:S(2)}) collective-permute-start(bf16[160,1536]{1,0:T(8,128)(2,1)S(1)} %shard_map.41), channel_id=1, source_target_pairs={{0,4},{1,5},{2,6},{3,7},{4,0},{5,1},{6,2},{7,3},{8,12},{9,13},{10,... | collective-permute-start | bytes 1474568 | tf_op jit(solution)/shard_map/ppermute | solution.py:414
  41.8 19.0 %collective-permute-start.15 = (bf16[160,1536]{1,0:T(8,128)(2,1)S(1)}, bf16[160,1536]{1,0:T(8,128)(2,1)S(1)}, u32[]{:S(2)}, u32[]{:S(2)}) collective-permute-start(bf16[160,1536]{1,0:T(8,128)(2,1)S(1)} %select_convert_fusion.refs_0_), channel_id=1, source_target_pairs={{0,1},{1,0},{2,3},{3,2},{4,5},{5,4},{6,7},{7,6},{8,9},{9,8},{10,11... | collective-permute-start | bytes 1474568 | tf_op jit(solution)/shard_map/ppermute | solution.py:414
  41.9 19.0 %collective-permute-start.16 = (bf16[160,1536]{1,0:T(8,128)(2,1)S(1)}, bf16[160,1536]{1,0:T(8,128)(2,1)S(1)}, u32[]{:S(2)}, u32[]{:S(2)}) collective-permute-start(bf16[160,1536]{1,0:T(8,128)(2,1)S(1)} %collective-permute-done.10.refs_1_.refs_2_), channel_id=1, source_target_pairs={{0,1},{1,0},{2,3},{3,2},{4,5},{5,4},{6,7},{7,6},{8,9},{9,8},{10,11... | collective-permute-start | bytes 1474568 | tf_op jit(solution)/shard_map/ppermute | solution.py:414
  53.7 11.3 %collective-permute-start.14 = (f32[160,512]{1,0:T(8,128)S(1)}, f32[160,512]{1,0:T(8,128)}, u32[]{:S(2)}, u32[]{:S(2)}) collective-permute-start(f32[160,512]{1,0:T(8,128)S(1)} %shard_map.43), channel_id=1, source_target_pairs={{0,8},{1,9},{2,10},{3,11},{4,12},{5,13},{6,14},{7,15},{8,0},{9,1},... | collective-permute-start | bytes 983048 | tf_op jit(solution)/shard_map/ppermute | solution.py:414
  53.7 11.3 %collective-permute-start.13 = (f32[160,512]{1,0:T(8,128)S(1)}, f32[160,512]{1,0:T(8,128)S(1)}, u32[]{:S(2)}, u32[]{:S(2)}) collective-permute-start(f32[160,512]{1,0:T(8,128)S(1)} %shard_map.43), channel_id=1, source_target_pairs={{0,4},{1,5},{2,6},{3,7},{4,0},{5,1},{6,2},{7,3},{8,12},{9,13},{10,... | collective-permute-start | bytes 983048 | tf_op jit(solution)/shard_map/ppermute | solution.py:414
  57.6 8.9 %collective-permute-start.12 = (bf16[160,1536]{1,0:T(8,128)(2,1)S(1)}, bf16[160,1536]{1,0:T(8,128)(2,1)S(1)}, u32[]{:S(2)}, u32[]{:S(2)}) collective-permute-start(bf16[160,1536]{1,0:T(8,128)(2,1)S(1)} %select_select_fusion.refs_1_.first.refs_0_.refs_4_), channel_id=1, source_target_pairs={{0,2},{1,3},{2,0},{3,1},{4,6},{5,7},{6,4},{7,5},{8,10},{9,11},{10,... | collective-permute-start | bytes 1474568 | tf_op jit(solution)/shard_map/ppermute | solution.py:414
  66.5 10.4 %collective-permute-start.19 = (f32[160,512]{1,0:T(8,128)}, f32[160,512]{1,0:T(8,128)}, u32[]{:S(2)}, u32[]{:S(2)}) collective-permute-start(f32[160,512]{1,0:T(8,128)} %collective-permute-done.14.refs_2_), channel_id=1, source_target_pairs={{0,4},{1,5},{2,6},{3,7},{4,0},{5,1},{6,2},{7,3},{8,12},{9,13},{10,... | collective-permute-start | bytes 983048 | tf_op jit(solution)/shard_map/ppermute | solution.py:414
  71.1 10.5 %collective-permute-start.18 = (f32[168,512]{1,0:T(8,128)S(1)}, f32[168,512]{1,0:T(8,128)S(1)}, u32[]{:S(2)}, u32[]{:S(2)}) collective-permute-start(f32[168,512]{1,0:T(8,128)S(1)} %shard_map.47.refs_0_.refs_8_), channel_id=1, source_target_pairs={{0,16},{16,0},{1,17},{17,1},{2,18},{18,2},{3,19},{19,3},{4,20},{20... | collective-permute-start | bytes 1032200 | tf_op jit(solution)/shard_map/ppermute | solution.py:417
  81.8 16.4 %collective-permute-start.20 = (f32[320,512]{1,0:T(8,128)S(1)}, f32[320,512]{1,0:T(8,128)S(1)}, u32[]{:S(2)}, u32[]{:S(2)}) collective-permute-start(f32[320,512]{1,0:T(8,128)S(1)} %shard_map.50.refs_1_), channel_id=1, source_target_pairs={{0,16},{16,0},{1,17},{17,1},{2,18},{18,2},{3,19},{19,3},{4,20},{20... | collective-permute-start | bytes 1966088 | tf_op jit(solution)/shard_map/ppermute | solution.py:417
  83.5 9.1 %collective-permute-start.24 = (f32[160,512]{1,0:T(8,128)S(1)}, f32[160,512]{1,0:T(8,128)S(1)}, u32[]{:S(2)}, u32[]{:S(2)}) collective-permute-start(f32[160,512]{1,0:T(8,128)S(1)} %shard_map.51.refs_5_.refs_1_), channel_id=1, source_target_pairs={{0,2},{1,3},{2,0},{3,1},{4,6},{5,7},{6,4},{7,5},{8,10},{9,11},{10,... | collective-permute-start | bytes 983048 | tf_op jit(solution)/shard_map/ppermute | solution.py:414
  85.2 14.7 %collective-permute-start.23 = (f32[160,512]{1,0:T(8,128)S(1)}, f32[160,512]{1,0:T(8,128)S(1)}, u32[]{:S(2)}, u32[]{:S(2)}) collective-permute-start(f32[160,512]{1,0:T(8,128)S(1)} %shard_map.51.refs_5_.refs_1_), channel_id=1, source_target_pairs={{0,1},{1,0},{2,3},{3,2},{4,5},{5,4},{6,7},{7,6},{8,9},{9,8},{10,11... | collective-permute-start | bytes 983048 | tf_op jit(solution)/shard_map/ppermute | solution.py:414
  98.2 19.0 %collective-permute-start.21 = (f32[320,640]{1,0:T(8,128)S(1)}, f32[320,640]{1,0:T(8,128)S(1)}, u32[]{:S(2)}, u32[]{:S(2)}) collective-permute-start(f32[320,640]{1,0:T(8,128)S(1)} %shard_map.53), channel_id=1, source_target_pairs={{0,16},{16,0},{1,17},{17,1},{2,18},{18,2},{3,19},{19,3},{4,20},{20... | collective-permute-start | bytes 2457608 | tf_op jit(solution)/shard_map/ppermute | solution.py:417
  106.2 15.9 %collective-permute-start.26 = (f32[320,512]{1,0:T(8,128)S(1)}, f32[320,512]{1,0:T(8,128)S(1)}, u32[]{:S(2)}, u32[]{:S(2)}) collective-permute-start(f32[320,512]{1,0:T(8,128)S(1)} %shard_map.58.refs_2_.refs_4_), channel_id=1, source_target_pairs={{0,1},{1,0},{2,3},{3,2},{4,5},{5,4},{6,7},{7,6},{8,9},{9,8},{10,11... | collective-permute-start | bytes 1966088 | tf_op jit(solution)/shard_map/ppermute | solution.py:414
  106.3 21.5 %collective-permute-start.30 = (f32[320,512]{1,0:T(8,128)S(1)}, f32[320,512]{1,0:T(8,128)S(1)}, u32[]{:S(2)}, u32[]{:S(2)}) collective-permute-start(f32[320,512]{1,0:T(8,128)S(1)} %shard_map.58.refs_2_.refs_4_), channel_id=1, source_target_pairs={{0,2},{1,3},{2,0},{3,1},{4,6},{5,7},{6,4},{7,5},{8,10},{9,11},{10,... | collective-permute-start | bytes 1966088 | tf_op jit(solution)/shard_map/ppermute | solution.py:414
  118.7 10.0 %collective-permute-start.27 = (f32[160,320]{1,0:T(8,128)S(1)}, f32[160,320]{1,0:T(8,128)S(1)}, u32[]{:S(2)}, u32[]{:S(2)}) collective-permute-start(f32[160,320]{1,0:T(8,128)S(1)} %get-tuple-element.32), channel_id=1, source_target_pairs={{0,2},{1,3},{2,0},{3,1},{4,6},{5,7},{6,4},{7,5},{8,10},{9,11},{10,... | collective-permute-start | bytes 614408 | tf_op jit(solution)/shard_map/ppermute | solution.py:414
  120.6 8.1 %collective-permute-start.22 = (f32[160,512]{1,0:T(8,128)S(1)}, f32[160,512]{1,0:T(8,128)S(1)}, u32[]{:S(2)}, u32[]{:S(2)}) collective-permute-start(f32[160,512]{1,0:T(8,128)S(1)} %shard_map.55.refs_0_), channel_id=1, source_target_pairs={{0,16},{16,0},{1,17},{17,1},{2,18},{18,2},{3,19},{19,3},{4,20},{20... | collective-permute-start | bytes 983048 | tf_op jit(solution)/shard_map/ppermute | solution.py:417
  127.8 9.9 %collective-permute-start.31 = (f32[320,512]{1,0:T(8,128)S(1)}, f32[320,512]{1,0:T(8,128)S(1)}, u32[]{:S(2)}, u32[]{:S(2)}) collective-permute-start(f32[320,512]{1,0:T(8,128)S(1)} %shard_map.63.refs_6_), channel_id=1, source_target_pairs={{0,1},{1,0},{2,3},{3,2},{4,5},{5,4},{6,7},{7,6},{8,9},{9,8},{10,11... | collective-permute-start | bytes 1966088 | tf_op jit(solution)/shard_map/ppermute | solution.py:414
  127.9 9.8 %collective-permute-start.28 = (f32[160,320]{1,0:T(8,128)S(1)}, f32[160,320]{1,0:T(8,128)S(1)}, u32[]{:S(2)}, u32[]{:S(2)}) collective-permute-start(f32[160,320]{1,0:T(8,128)S(1)} %get-tuple-element.24.refs_1_.refs_2_), channel_id=1, source_target_pairs={{0,1},{1,0},{2,3},{3,2},{4,5},{5,4},{6,7},{7,6},{8,9},{9,8},{10,11... | collective-permute-start | bytes 614408 | tf_op jit(solution)/shard_map/ppermute | solution.py:414
  128.4 9.3 %collective-permute-start.29 = (f32[160,320]{1,0:T(8,128)S(1)}, f32[160,320]{1,0:T(8,128)S(1)}, u32[]{:S(2)}, u32[]{:S(2)}) collective-permute-start(f32[160,320]{1,0:T(8,128)S(1)} %get-tuple-element.38), channel_id=1, source_target_pairs={{0,3},{1,2},{2,1},{3,0},{4,7},{5,6},{6,5},{7,4},{8,11},{9,10},{10,... | collective-permute-start | bytes 614408 | tf_op jit(solution)/shard_map/ppermute | solution.py:414
  (28 other events, 180.1 us)

commit v2 on v1

--- a/solution.py
+++ b/solution.py
@@ -161,7 +161,7 @@
         out_specs=[VMEM] * len(out_shape),
         scratch_shapes=scratch,
         compiler_params=room(*out_shape, f32(2 * size, size), *squares),
-        cost_estimate=cost(6_000_000_000),
+        cost_estimate=cost(3_500_000_000),
     )(place, *squares, *waits)
 
 
@@ -257,27 +257,35 @@
     )(*parts, rel)
 
 
-def side_kernel(n_parts, n_rel, scale, *refs):
-    parts, rel, out = refs[:n_parts], refs[n_parts : n_parts + n_rel], refs[-1]
+def side_kernel(n_got, n_rel, scale, keep, *refs):
+    rel, out = refs[-1 - n_rel : -1], refs[-1]
+    got = refs[: -1 - n_rel]
     own = rel[0].shape[0]
     factor = scale[0:1, 0:1]
+    each = n_rel // n_got
     for n in range(n_rel):
         cut = slice(n * own, (n + 1) * own)
-        value = parts[0][cut, :]
-        for x in parts[1:]:
-            value = value + x[cut, :]
+        inside = slice((n % each) * own, (n % each + 1) * own)
+        value = keep[cut, :]
+        for x in got[n // each :: n_got]:
+            value = value + x[inside, :]
         out[cut, :] = rel[n][...] + value * factor
 
 
-def side_rows(scale, parts, rel, waits):
-    return pl.pallas_call(
-        functools.partial(side_kernel, len(parts), len(rel)),
-        out_shape=f32(*parts[0].shape),
-        in_specs=[VMEM] * (1 + len(parts) + len(rel)) + [ANYWHERE] * len(waits),
+def side_rows(scale, keep, n_got, got, rel, waits):
+    count = len(got)
+
+    def kernel(scale, keep, *refs):
+        side_kernel(n_got, len(rel), scale, keep, *refs[: count + len(rel)], refs[-1])
+
+    return pl.pallas_call(
+        kernel,
+        out_shape=f32(*keep.shape),
+        in_specs=[VMEM] * (2 + count + len(rel)) + [ANYWHERE] * len(waits),
         out_specs=VMEM,
-        compiler_params=room(*parts, *rel, parts[0]),
+        compiler_params=room(keep, keep, *got, *rel),
         cost_estimate=cost(1_000_000),
-    )(scale, *parts, *rel, *waits)
+    )(scale, keep, *got, *rel, *waits)
 
 
 def head_products(place, groups, head, waits):
@@ -498,27 +506,35 @@
         head.append(rows_xor(head[2], 1))
         rows = message(place, scale_part.reshape(1), first, head)
         rows_got = [snp_xor(rows, bits) for bits in range(1, n_snp)]
-        sides = head_products(place, groups, head, [rows])
+        halves = 2 if part % 2 == 0 else 1
+        split_groups = [
+            groups[b][h * part // halves : (h + 1) * part // halves]
+            for b in range(1, n_snp)
+            for h in range(halves)
+        ]
+        keep, *out = head_products(place, groups[:1] + split_groups, head, [rows])
+        rel_line[-1] = after(rel_line[-1], out[0])
         total, scale = total_rows([rows] + rows_got, select_order(rel_line, z)[0])
-        sides = [sides[0]] + [after(x, total) for x in sides[1:]]
-        side_got = [snp_xor(sides[bits], bits) for bits in range(1, n_snp)]
-        total = after(total, *sides[1:])
+        out = [after(x, total) for x in out]
+        side_got = [snp_xor(x, n // halves + 1) for n, x in enumerate(out)]
+        early = side_got[::halves]
+        total = after(total, *out)
 
         (lead,) = head_products(place, [[centered]], head, [total])
         diagonal = [total, rows_xor(total, 1)]
-        diagonal.append(after(rows_xor(total, 2), lead))
+        diagonal.append(after(rows_xor(total, 2), lead, *early))
         diagonal.append(rows_xor(diagonal[2], 1))
 
         gram_got = [
-            snp_xor(after(leaving[b - 1], *side_got), b) for b in range(1, n_snp)
+            snp_xor(after(leaving[b - 1], *early), b) for b in range(1, n_snp)
         ]
         pieces = gram_products(plane, groups[0], gram_got, [])
         moved = [pieces[0]] + [rows_xor(pieces[k], k) for k in range(1, GROUP)]
 
-        inv, column, square = factor_step(place, diagonal, PANEL, side_got)
+        inv, column, square = factor_step(place, diagonal, PANEL, [])
         inverses, below = [inv], [column]
         rel_side = select_order(rel_line, z ^ (col * part))[:part]
-        side = side_rows(scale, [sides[0]] + side_got, rel_side, [inverses[0]])
+        side = side_rows(scale, keep, halves, side_got, rel_side, [inverses[0]])
         sides = [side, rows_xor(side, 1), rows_xor(side, 2)]
 
         lead = after(lead, pieces[1])

time: 141 us -> 150 us (1.064)
  waiting for transfers between devices: 57.8 us -> 66.7 us
    ppermute x4 -> x5, waiting for transfers between devices: 8.92 us -> 16.6 us  [snp_xor(): return lax.ppermute(x, 'snp', [(s, s ^ bits) for s in range(n_snp)])]
    ppermute x27, starting transfers between devices: 22.6 us -> 21 us  [rows_xor(): return lax.ppermute(x, 'rows', [(r, r ^ bits) for r in range(n_rows)])]
    ppermute x4 -> x5, starting transfers between devices: 6.46 us -> 6.95 us  [snp_xor(): return lax.ppermute(x, 'snp', [(s, s ^ bits) for s in range(n_snp)])]
  transfers between devices with their start and end apart: 32 -> 33, of which waited for: 15 -> 17; matrix products, arithmetic and copies ran while one was open for 3% -> 3% of each run, Pallas kernels for 27% -> 26%
where the time goes in v2:
time: 150 us
  waiting for transfers between devices  66.7 us (44%)
  Pallas kernels  42 us (28%)
  starting transfers between devices  31.4 us (21%)
  other arithmetic  6.4 us (4%)
  between operations  2.31 us (2%)
    ppermute x27, waiting for transfers between devices, rows_xor(): return lax.ppermute(x, 'rows', [(r, r ^ bits) for r in range(n_rows)])  49.9 us
    pallas_call x4, Pallas kernels, factor_step(): pl.pallas_call(kernel, out_shape=out_shape, in_specs=[SMEM] + [VMEM] * n_...  22.4 us
    ppermute x27, starting transfers between devices, rows_xor(): return lax.ppermute(x, 'rows', [(r, r ^ bits) for r in range(n_rows)])  21 us
    ppermute x5, waiting for transfers between devices, snp_xor(): return lax.ppermute(x, 'snp', [(s, s ^ bits) for s in range(n_snp)])  16.6 us
    ppermute x5, starting transfers between devices, snp_xor(): return lax.ppermute(x, 'snp', [(s, s ^ bits) for s in range(n_snp)])  6.95 us
    pallas_call x2, Pallas kernels, head_products(): pl.pallas_call(functools.partial(head_kernel, len(left), sizes), out_shap...  5.48 us
    pallas_call x1, Pallas kernels, solve(): pl.pallas_call(functools.partial(solve_kernel, len(inverses), len(lead)),...  4.41 us
    select_n x3, other arithmetic, select_order(): jnp.where(swap, blocks[k ^ bit], blocks[k])  3.84 us
  transfers between devices with their start and end apart: 33, of which 17 were waited for; matrix products, arithmetic and copies ran while one was open for 3% of the time, Pallas kernels for 26%

profile of v2, /device:TPU:0, one launch (start us, length us, event | category | flops | bytes accessed | tf_op | source)
XLA Modules:
  0.0 149.9 jit_solution(18225476927870212059)
XLA Ops:
  2.2 3.0 %collective-permute-start.1 = (f32[2,1536]{1,0:T(2,128)S(1)}, f32[2,1536]{1,0:T(2,128)S(1)}, u32[]{:S(2)}, u32[]{:S(2)}) collective-permute-start(f32[2,1536]{1,0:T(2,128)S(1)} %pad_maximum_fusion), channel_id=1, source_target_pairs={{0,2},{1,3},{2,0},{3,1},{4,6},{5,7},{6,4},{7,5},{8,10},{9,11},{10,... | collective-permute-start | bytes 36872 | tf_op jit(solution)/shard_map/ppermute | solution.py:422
  8.4 3.7 %collective-permute-start.5 = (f32[2,1536]{1,0:T(2,128)S(1)}, f32[2,1536]{1,0:T(2,128)S(1)}, u32[]{:S(2)}, u32[]{:S(2)}) collective-permute-start(f32[2,1536]{1,0:T(2,128)S(1)} %add_add_fusion.1), channel_id=1, source_target_pairs={{0,12},{1,13},{2,14},{3,15},{4,8},{5,9},{6,10},{7,11},{8,4},{9,5},... | collective-permute-start | bytes 36872 | tf_op jit(solution)/shard_map/ppermute | solution.py:422
  12.9 3.4 %collective-permute-start.7 = (f32[160,512]{1,0:T(8,128)S(1)}, f32[160,512]{1,0:T(8,128)S(1)}, u32[]{:S(2)}, u32[]{:S(2)}) collective-permute-start(f32[160,512]{1,0:T(8,128)S(1)} %slice.11), channel_id=1, source_target_pairs={{0,16},{1,17},{2,18},{3,19},{4,20},{5,21},{6,22},{7,23},{8,24},{9,... | collective-permute-start | bytes 983048 | tf_op jit(solution)/shard_map/ppermute | solution.py:430
  18.5 2.9 %collective-permute-start.6 = (bf16[160,1536]{1,0:T(8,128)(2,1)S(1)}, bf16[160,1536]{1,0:T(8,128)(2,1)S(1)}, u32[]{:S(2)}, u32[]{:S(2)}) collective-permute-start(bf16[160,1536]{1,0:T(8,128)(2,1)S(1)} %select_convert_fusion.refs_0_), channel_id=1, source_target_pairs={{0,8},{1,9},{2,10},{3,11},{4,12},{5,13},{6,14},{7,15},{8,0},{9,1},... | collective-permute-start | bytes 1474568 | tf_op jit(solution)/shard_map/ppermute | solution.py:422
  22.4 16.9 %collective-permute-done.8.refs_2_ = bf16[160,1536]{1,0:T(8,128)(2,1)S(1)} collective-permute-done((bf16[160,1536]{1,0:T(8,128)(2,1)S(1)}, bf16[160,1536]{1,0:T(8,128)(2,1)S(1)}, u32[]{:S(2)}, u32[]{:S(2)}) %collective-permute-start.8) | collective-permute-done | bytes 491552 | tf_op jit(solution)/shard_map/ppermute | solution.py:422
  39.3 2.4 %collective-permute-done.6.refs_0_ = bf16[160,1536]{1,0:T(8,128)(2,1)S(1)} collective-permute-done((bf16[160,1536]{1,0:T(8,128)(2,1)S(1)}, bf16[160,1536]{1,0:T(8,128)(2,1)S(1)}, u32[]{:S(2)}, u32[]{:S(2)}) %collective-permute-start.6) | collective-permute-done | bytes 491552 | tf_op jit(solution)/shard_map/ppermute | solution.py:422
  42.5 11.3 %collective-permute-done.9.refs_0_ = bf16[160,1536]{1,0:T(8,128)(2,1)S(1)} collective-permute-done((bf16[160,1536]{1,0:T(8,128)(2,1)S(1)}, bf16[160,1536]{1,0:T(8,128)(2,1)S(1)}, u32[]{:S(2)}, u32[]{:S(2)}) %collective-permute-start.9) | collective-permute-done | bytes 491552 | tf_op jit(solution)/shard_map/ppermute | solution.py:422
  53.8 2.4 %collective-permute-start.13 = (f32[160,512]{1,0:T(8,128)S(1)}, f32[160,512]{1,0:T(8,128)S(1)}, u32[]{:S(2)}, u32[]{:S(2)}) collective-permute-start(f32[160,512]{1,0:T(8,128)S(1)} %shard_map.43), channel_id=1, source_target_pairs={{0,4},{1,5},{2,6},{3,7},{4,0},{5,1},{6,2},{7,3},{8,12},{9,13},{10,... | collective-permute-start | bytes 983048 | tf_op jit(solution)/shard_map/ppermute | solution.py:422
  62.3 2.8 %collective-permute-done.14.refs_2_ = f32[160,512]{1,0:T(8,128)} collective-permute-done((f32[160,512]{1,0:T(8,128)S(1)}, f32[160,512]{1,0:T(8,128)}, u32[]{:S(2)}, u32[]{:S(2)}) %collective-permute-start.14) | collective-permute-done | bytes 327712 | tf_op jit(solution)/shard_map/ppermute | solution.py:422
  68.5 2.7 %shard_map.47.refs_8_.refs_0_ = f32[168,512]{1,0:T(8,128)S(1)} custom-call(s32[2]{0:T(128)S(1)} %pad_add_fusion.place.refs_0_, f32[1]{0:T(128)} %bitcast.2.scale, bf16[160,1536]{1,0:T(8,128)(2,1)S(1)} %select_select_fusion.refs_1_.first.refs_0_.refs_4_, bf16[160,1536]{1,0:T(8,128)(2,1)S(1)} %select_select_fusion.refs_1_.first.refs_0_.refs_4_, ...), custom_call_target="tpu_custom_call" | custom-call | flops 251658240 | bytes 131072 | tf_op jit(solution)/shard_map/pallas_call | solution.py:227
  73.0 3.5 %shard_map.48 = (f32[320,512]{1,0:T(8,128)S(1)}, f32[160,512]{1,0:T(8,128)S(1)}, f32[160,512]{1,0:T(8,128)S(1)}) custom-call(s32[2]{0:T(128)S(1)} %pad_add_fusion.place.refs_0_, bf16[160,1536]{1,0:T(8,128)(2,1)S(1)} %copy-done.1, bf16[160,1536]{1,0:T(8,128)(2,1)S(1)} %copy-done, bf16[160,1536]{1,0:T(8,128)(2,1)S(1)} %copy-done.5, ...), custom_call_target="tpu_custom_call" | custom-call | flops 1006632960 | bytes 131072 | tf_op jit(solution)/shard_map/pallas_call | solution.py:295
  79.1 2.3 %collective-permute-done.18.refs_1_ = f32[168,512]{1,0:T(8,128)S(1)} collective-permute-done((f32[168,512]{1,0:T(8,128)S(1)}, f32[168,512]{1,0:T(8,128)S(1)}, u32[]{:S(2)}, u32[]{:S(2)}) %collective-permute-start.18) | collective-permute-done | bytes 344096 | tf_op jit(solution)/shard_map/ppermute | solution.py:425
  83.2 1.7 %collective-permute-start.20 = (f32[160,512]{1,0:T(8,128)S(1)}, f32[160,512]{1,0:T(8,128)S(1)}, u32[]{:S(2)}, u32[]{:S(2)}) collective-permute-start(f32[160,512]{1,0:T(8,128)S(1)} %shard_map.51.refs_1_), channel_id=1, source_target_pairs={{0,16},{16,0},{1,17},{17,1},{2,18},{18,2},{3,19},{19,3},{4,20},{20... | collective-permute-start | bytes 983048 | tf_op jit(solution)/shard_map/ppermute | solution.py:425
  84.9 2.0 %shard_map.54.refs_0_.refs_1_ = f32[160,512]{1,0:T(8,128)S(1)} custom-call(s32[2]{0:T(128)S(1)} %pad_add_fusion.place.refs_0_, bf16[160,1536]{1,0:T(8,128)(2,1)S(1)} %select_convert_fusion.refs_0_, bf16[160,1536]{1,0:T(8,128)(2,1)S(1)} %select_select_fusion.refs_1_.first.refs_0_.refs_4_, bf16[160,1536]{1,0:T(8,128)(2,1)} %collective-permute-done.11.refs_1_.refs_5_.refs_2_, ...), custom_call_target="tpu_custom_call" | custom-call | flops 251658240 | bytes 131072 | tf_op jit(solution)/shard_map/pallas_call | solution.py:295
  86.9 3.8 %collective-permute-done.24.refs_0_ = f32[160,512]{1,0:T(8,128)S(1)} collective-permute-done((f32[160,512]{1,0:T(8,128)S(1)}, f32[160,512]{1,0:T(8,128)S(1)}, u32[]{:S(2)}, u32[]{:S(2)}) %collective-permute-start.24) | collective-permute-done | bytes 327712 | tf_op jit(solution)/shard_map/ppermute | solution.py:422
  94.2 6.2 %shard_map.59 = (f32[128,128]{1,0:T(8,128)S(1)}, f32[384,128]{1,0:T(8,128)S(1)}, f32[384,384]{1,0:T(8,128)S(1)}) custom-call(s32[2]{0:T(128)S(1)} %pad_add_fusion.place.refs_0_, f32[160,512]{1,0:T(8,128)S(1)} %shard_map.53.refs_5_.refs_1_, f32[160,512]{1,0:T(8,128)S(1)} %collective-permute-done.23.refs_2_, f32[160,512]{1,0:T(8,128)S(1)} %shard_map.58.refs_3_, ...), custom_call_target="tpu_custom_call" | custom-call | flops 3500000000 | bytes 131072 | tf_op jit(solution)/shard_map/pallas_call | solution.py:157
  100.4 2.3 %collective-permute-done.26.refs_1_ = f32[160,512]{1,0:T(8,128)S(1)} collective-permute-done((f32[160,512]{1,0:T(8,128)S(1)}, f32[160,512]{1,0:T(8,128)S(1)}, u32[]{:S(2)}, u32[]{:S(2)}) %collective-permute-start.26) | collective-permute-done | bytes 327712 | tf_op jit(solution)/shard_map/ppermute | solution.py:425
  103.3 5.9 %shard_map.61 = (f32[128,128]{1,0:T(8,128)S(1)}, f32[256,128]{1,0:T(8,128)S(1)}, f32[256,256]{1,0:T(8,128)S(1)}) custom-call(s32[2]{0:T(128)S(1)} %pad_add_fusion.place.refs_0_, f32[384,384]{1,0:T(8,128)S(1)} %get-tuple-element.28.refs_1_, f32[320,512]{1,0:T(8,128)S(1)} %shard_map.60.refs_2_.refs_4_), custom_call_target="tpu_custom_call" | custom-call | flops 3500000000 | bytes 131072 | tf_op jit(solution)/shard_map/pallas_call | solution.py:157
  109.2 10.6 %collective-permute-done.21.refs_6_ = f32[320,640]{1,0:T(8,128)S(1)} collective-permute-done((f32[320,640]{1,0:T(8,128)S(1)}, f32[320,640]{1,0:T(8,128)S(1)}, u32[]{:S(2)}, u32[]{:S(2)}) %collective-permute-start.21) | collective-permute-done | bytes 819232 | tf_op jit(solution)/shard_map/ppermute | solution.py:425
  122.8 5.7 %shard_map.62 = (f32[128,128]{1,0:T(8,128)S(1)}, f32[128,128]{1,0:T(8,128)S(1)}, f32[128,128]{1,0:T(8,128)S(1)}) custom-call(s32[2]{0:T(128)S(1)} %pad_add_fusion.place.refs_0_, f32[256,256]{1,0:T(8,128)S(1)} %get-tuple-element.31.refs_1_, f32[160,320]{1,0:T(8,128)S(1)} %get-tuple-element.26.refs_1_.refs_2_, ...), custom_call_target="tpu_custom_call" | custom-call | flops 3500000000 | bytes 131072 | tf_op jit(solution)/shard_map/pallas_call | solution.py:157
  130.8 6.6 %collective-permute-done.28.refs_3_.refs_2_ = f32[160,320]{1,0:T(8,128)S(1)} collective-permute-done((f32[160,320]{1,0:T(8,128)S(1)}, f32[160,320]{1,0:T(8,128)S(1)}, u32[]{:S(2)}, u32[]{:S(2)}) %collective-permute-start.28) | collective-permute-done | bytes 204832 | tf_op jit(solution)/shard_map/ppermute | solution.py:422
  137.4 4.5 %shard_map.63.refs_5_ = f32[128,128]{1,0:T(8,128)S(1)} custom-call(s32[2]{0:T(128)S(1)} %pad_add_fusion.place.refs_0_, f32[128,128]{1,0:T(8,128)S(1)} %get-tuple-element.33.refs_1_, f32[160,512]{1,0:T(8,128)S(1)} %collective-permute-done.22.refs_2_.refs_1_, f32[160,320]{1,0:T(8,128)S(1)} %collective-permute-done.28.refs_3_.refs_2_), custom_call_target="tpu_custom_call" | custom-call | flops 3500000000 | bytes 131072 | tf_op jit(solution)/shard_map/pallas_call | solution.py:157
  142.0 4.4 %shard_map.64 = (f32[160,512]{1,0:T(8,128)}, f32[160,512]{1,0:T(8,128)S(1)}) custom-call(f32[160,512]{1,0:T(8,128)S(1)} %select_add_fusion.refs_1_.rel, f32[8,128]{1,0:T(8,128)S(1)} %get-tuple-element.23.scale, f32[160,512]{1,0:T(8,128)S(1)} %shard_map.57.refs_0_, f32[160,512]{1,0:T(8,128)S(1)} %collective-permute-done.22.refs_2_.refs_1_, ...), custom_call_target="tpu_custom_call" | custom-call | flops 167772160 | bytes 131072 | tf_op jit(solution)/shard_map/pallas_call | solution.py:195
  146.4 3.5 %shard_map.66 = f32[160,1280]{1,0:T(8,128)} custom-call(s32[2]{0:T(128)S(1)} %pad_add_fusion.place.refs_0_, f32[8,128]{1,0:T(8,128)S(1)} %get-tuple-element.23.scale, f32[160,1280]{1,0:T(8,128)S(1)} %copy-done.11, f32[160,512]{1,0:T(8,128)S(1)} %get-tuple-element.38.weights, f32[160,320]{1,0:T(8,128)S(1)} %get-tuple-element.39.refs_0_, ...), custom_call_target="tpu_custom_call" | custom-call | flops 209715200 | bytes 131072 | tf_op jit(solution)/shard_map/pallas_call | solution.py:376
  (124 shorter events, 33.2 us)
Async XLA Ops:
  12.9 9.4 %collective-permute-start.7 = (f32[160,512]{1,0:T(8,128)S(1)}, f32[160,512]{1,0:T(8,128)S(1)}, u32[]{:S(2)}, u32[]{:S(2)}) collective-permute-start(f32[160,512]{1,0:T(8,128)S(1)} %slice.11), channel_id=1, source_target_pairs={{0,16},{1,17},{2,18},{3,19},{4,20},{5,21},{6,22},{7,23},{8,24},{9,... | collective-permute-start | bytes 983048 | tf_op jit(solution)/shard_map/ppermute | solution.py:430
  17.5 21.8 %collective-permute-start.8 = (bf16[160,1536]{1,0:T(8,128)(2,1)S(1)}, bf16[160,1536]{1,0:T(8,128)(2,1)S(1)}, u32[]{:S(2)}, u32[]{:S(2)}) collective-permute-start(bf16[160,1536]{1,0:T(8,128)(2,1)S(1)} %select_convert_fusion.refs_0_), channel_id=1, source_target_pairs={{0,4},{1,5},{2,6},{3,7},{4,0},{5,1},{6,2},{7,3},{8,12},{9,13},{10,... | collective-permute-start | bytes 1474568 | tf_op jit(solution)/shard_map/ppermute | solution.py:422
  18.5 23.1 %collective-permute-start.6 = (bf16[160,1536]{1,0:T(8,128)(2,1)S(1)}, bf16[160,1536]{1,0:T(8,128)(2,1)S(1)}, u32[]{:S(2)}, u32[]{:S(2)}) collective-permute-start(bf16[160,1536]{1,0:T(8,128)(2,1)S(1)} %select_convert_fusion.refs_0_), channel_id=1, source_target_pairs={{0,8},{1,9},{2,10},{3,11},{4,12},{5,13},{6,14},{7,15},{8,0},{9,1},... | collective-permute-start | bytes 1474568 | tf_op jit(solution)/shard_map/ppermute | solution.py:422
  21.4 20.5 %collective-permute-start.10 = (bf16[160,1536]{1,0:T(8,128)(2,1)S(1)}, bf16[160,1536]{1,0:T(8,128)(2,1)S(1)}, u32[]{:S(2)}, u32[]{:S(2)}) collective-permute-start(bf16[160,1536]{1,0:T(8,128)(2,1)S(1)} %select_convert_fusion.refs_0_), channel_id=1, source_target_pairs={{0,2},{1,3},{2,0},{3,1},{4,6},{5,7},{6,4},{7,5},{8,10},{9,11},{10,... | collective-permute-start | bytes 1474568 | tf_op jit(solution)/shard_map/ppermute | solution.py:422
  41.6 12.1 %collective-permute-start.9 = (bf16[160,1536]{1,0:T(8,128)(2,1)S(1)}, bf16[160,1536]{1,0:T(8,128)(2,1)S(1)}, u32[]{:S(2)}, u32[]{:S(2)}) collective-permute-start(bf16[160,1536]{1,0:T(8,128)(2,1)S(1)} %shard_map.41), channel_id=1, source_target_pairs={{0,4},{1,5},{2,6},{3,7},{4,0},{5,1},{6,2},{7,3},{8,12},{9,13},{10,... | collective-permute-start | bytes 1474568 | tf_op jit(solution)/shard_map/ppermute | solution.py:422
  41.9 19.0 %collective-permute-start.15 = (bf16[160,1536]{1,0:T(8,128)(2,1)S(1)}, bf16[160,1536]{1,0:T(8,128)(2,1)S(1)}, u32[]{:S(2)}, u32[]{:S(2)}) collective-permute-start(bf16[160,1536]{1,0:T(8,128)(2,1)S(1)} %select_convert_fusion.refs_0_), channel_id=1, source_target_pairs={{0,1},{1,0},{2,3},{3,2},{4,5},{5,4},{6,7},{7,6},{8,9},{9,8},{10,11... | collective-permute-start | bytes 1474568 | tf_op jit(solution)/shard_map/ppermute | solution.py:422
  41.9 19.0 %collective-permute-start.16 = (bf16[160,1536]{1,0:T(8,128)(2,1)S(1)}, bf16[160,1536]{1,0:T(8,128)(2,1)S(1)}, u32[]{:S(2)}, u32[]{:S(2)}) collective-permute-start(bf16[160,1536]{1,0:T(8,128)(2,1)S(1)} %collective-permute-done.10.refs_1_.refs_2_), channel_id=1, source_target_pairs={{0,1},{1,0},{2,3},{3,2},{4,5},{5,4},{6,7},{7,6},{8,9},{9,8},{10,11... | collective-permute-start | bytes 1474568 | tf_op jit(solution)/shard_map/ppermute | solution.py:422
  53.8 11.3 %collective-permute-start.14 = (f32[160,512]{1,0:T(8,128)S(1)}, f32[160,512]{1,0:T(8,128)}, u32[]{:S(2)}, u32[]{:S(2)}) collective-permute-start(f32[160,512]{1,0:T(8,128)S(1)} %shard_map.43), channel_id=1, source_target_pairs={{0,8},{1,9},{2,10},{3,11},{4,12},{5,13},{6,14},{7,15},{8,0},{9,1},... | collective-permute-start | bytes 983048 | tf_op jit(solution)/shard_map/ppermute | solution.py:422
  53.8 11.3 %collective-permute-start.13 = (f32[160,512]{1,0:T(8,128)S(1)}, f32[160,512]{1,0:T(8,128)S(1)}, u32[]{:S(2)}, u32[]{:S(2)}) collective-permute-start(f32[160,512]{1,0:T(8,128)S(1)} %shard_map.43), channel_id=1, source_target_pairs={{0,4},{1,5},{2,6},{3,7},{4,0},{5,1},{6,2},{7,3},{8,12},{9,13},{10,... | collective-permute-start | bytes 983048 | tf_op jit(solution)/shard_map/ppermute | solution.py:422
  57.6 8.9 %collective-permute-start.12 = (bf16[160,1536]{1,0:T(8,128)(2,1)S(1)}, bf16[160,1536]{1,0:T(8,128)(2,1)S(1)}, u32[]{:S(2)}, u32[]{:S(2)}) collective-permute-start(bf16[160,1536]{1,0:T(8,128)(2,1)S(1)} %select_select_fusion.refs_1_.first.refs_0_.refs_4_), channel_id=1, source_target_pairs={{0,2},{1,3},{2,0},{3,1},{4,6},{5,7},{6,4},{7,5},{8,10},{9,11},{10,... | collective-permute-start | bytes 1474568 | tf_op jit(solution)/shard_map/ppermute | solution.py:422
  66.5 10.4 %collective-permute-start.19 = (f32[160,512]{1,0:T(8,128)}, f32[160,512]{1,0:T(8,128)}, u32[]{:S(2)}, u32[]{:S(2)}) collective-permute-start(f32[160,512]{1,0:T(8,128)} %collective-permute-done.14.refs_2_), channel_id=1, source_target_pairs={{0,4},{1,5},{2,6},{3,7},{4,0},{5,1},{6,2},{7,3},{8,12},{9,13},{10,... | collective-permute-start | bytes 983048 | tf_op jit(solution)/shard_map/ppermute | solution.py:422
  71.3 10.2 %collective-permute-start.18 = (f32[168,512]{1,0:T(8,128)S(1)}, f32[168,512]{1,0:T(8,128)S(1)}, u32[]{:S(2)}, u32[]{:S(2)}) collective-permute-start(f32[168,512]{1,0:T(8,128)S(1)} %shard_map.47.refs_8_.refs_0_), channel_id=1, source_target_pairs={{0,16},{16,0},{1,17},{17,1},{2,18},{18,2},{3,19},{19,3},{4,20},{20... | collective-permute-start | bytes 1032200 | tf_op jit(solution)/shard_map/ppermute | solution.py:425
  81.5 9.1 %collective-permute-start.24 = (f32[160,512]{1,0:T(8,128)S(1)}, f32[160,512]{1,0:T(8,128)S(1)}, u32[]{:S(2)}, u32[]{:S(2)}) collective-permute-start(f32[160,512]{1,0:T(8,128)S(1)} %shard_map.53.refs_5_.refs_1_), channel_id=1, source_target_pairs={{0,2},{1,3},{2,0},{3,1},{4,6},{5,7},{6,4},{7,5},{8,10},{9,11},{10,... | collective-permute-start | bytes 983048 | tf_op jit(solution)/shard_map/ppermute | solution.py:422
  83.2 9.0 %collective-permute-start.20 = (f32[160,512]{1,0:T(8,128)S(1)}, f32[160,512]{1,0:T(8,128)S(1)}, u32[]{:S(2)}, u32[]{:S(2)}) collective-permute-start(f32[160,512]{1,0:T(8,128)S(1)} %shard_map.51.refs_1_), channel_id=1, source_target_pairs={{0,16},{16,0},{1,17},{17,1},{2,18},{18,2},{3,19},{19,3},{4,20},{20... | collective-permute-start | bytes 983048 | tf_op jit(solution)/shard_map/ppermute | solution.py:425
  84.9 9.3 %collective-permute-start.23 = (f32[160,512]{1,0:T(8,128)S(1)}, f32[160,512]{1,0:T(8,128)S(1)}, u32[]{:S(2)}, u32[]{:S(2)}) collective-permute-start(f32[160,512]{1,0:T(8,128)S(1)} %shard_map.53.refs_5_.refs_1_), channel_id=1, source_target_pairs={{0,1},{1,0},{2,3},{3,2},{4,5},{5,4},{6,7},{7,6},{8,9},{9,8},{10,11... | collective-permute-start | bytes 983048 | tf_op jit(solution)/shard_map/ppermute | solution.py:422
  92.1 10.5 %collective-permute-start.26 = (f32[160,512]{1,0:T(8,128)S(1)}, f32[160,512]{1,0:T(8,128)S(1)}, u32[]{:S(2)}, u32[]{:S(2)}) collective-permute-start(f32[160,512]{1,0:T(8,128)S(1)} %shard_map.52.refs_2_), channel_id=1, source_target_pairs={{0,16},{16,0},{1,17},{17,1},{2,18},{18,2},{3,19},{19,3},{4,20},{20... | collective-permute-start | bytes 983048 | tf_op jit(solution)/shard_map/ppermute | solution.py:425
  93.5 26.3 %collective-permute-start.21 = (f32[320,640]{1,0:T(8,128)S(1)}, f32[320,640]{1,0:T(8,128)S(1)}, u32[]{:S(2)}, u32[]{:S(2)}) collective-permute-start(f32[320,640]{1,0:T(8,128)S(1)} %shard_map.55), channel_id=1, source_target_pairs={{0,16},{16,0},{1,17},{17,1},{2,18},{18,2},{3,19},{19,3},{4,20},{20... | collective-permute-start | bytes 2457608 | tf_op jit(solution)/shard_map/ppermute | solution.py:425
  102.8 20.0 %collective-permute-start.27 = (f32[320,512]{1,0:T(8,128)S(1)}, f32[320,512]{1,0:T(8,128)S(1)}, u32[]{:S(2)}, u32[]{:S(2)}) collective-permute-start(f32[320,512]{1,0:T(8,128)S(1)} %shard_map.60.refs_2_.refs_4_), channel_id=1, source_target_pairs={{0,1},{1,0},{2,3},{3,2},{4,5},{5,4},{6,7},{7,6},{8,9},{9,8},{10,11... | collective-permute-start | bytes 1966088 | tf_op jit(solution)/shard_map/ppermute | solution.py:422
  102.9 25.7 %collective-permute-start.31 = (f32[320,512]{1,0:T(8,128)S(1)}, f32[320,512]{1,0:T(8,128)S(1)}, u32[]{:S(2)}, u32[]{:S(2)}) collective-permute-start(f32[320,512]{1,0:T(8,128)S(1)} %shard_map.60.refs_2_.refs_4_), channel_id=1, source_target_pairs={{0,2},{1,3},{2,0},{3,1},{4,6},{5,7},{6,4},{7,5},{8,10},{9,11},{10,... | collective-permute-start | bytes 1966088 | tf_op jit(solution)/shard_map/ppermute | solution.py:422
  121.3 16.1 %collective-permute-start.22 = (f32[160,512]{1,0:T(8,128)S(1)}, f32[160,512]{1,0:T(8,128)S(1)}, u32[]{:S(2)}, u32[]{:S(2)}) collective-permute-start(f32[160,512]{1,0:T(8,128)S(1)} %shard_map.57.refs_0_), channel_id=1, source_target_pairs={{0,16},{16,0},{1,17},{17,1},{2,18},{18,2},{3,19},{19,3},{4,20},{20... | collective-permute-start | bytes 983048 | tf_op jit(solution)/shard_map/ppermute | solution.py:425
  128.5 17.9 %collective-permute-start.32 = (f32[320,512]{1,0:T(8,128)S(1)}, f32[320,512]{1,0:T(8,128)S(1)}, u32[]{:S(2)}, u32[]{:S(2)}) collective-permute-start(f32[320,512]{1,0:T(8,128)S(1)} %shard_map.65.refs_6_), channel_id=1, source_target_pairs={{0,1},{1,0},{2,3},{3,2},{4,5},{5,4},{6,7},{7,6},{8,9},{9,8},{10,11... | collective-permute-start | bytes 1966088 | tf_op jit(solution)/shard_map/ppermute | solution.py:422
  128.6 8.8 %collective-permute-start.28 = (f32[160,320]{1,0:T(8,128)S(1)}, f32[160,320]{1,0:T(8,128)S(1)}, u32[]{:S(2)}, u32[]{:S(2)}) collective-permute-start(f32[160,320]{1,0:T(8,128)S(1)} %get-tuple-element.34), channel_id=1, source_target_pairs={{0,2},{1,3},{2,0},{3,1},{4,6},{5,7},{6,4},{7,5},{8,10},{9,11},{10,... | collective-permute-start | bytes 614408 | tf_op jit(solution)/shard_map/ppermute | solution.py:422
  129.1 17.4 %collective-permute-start.29 = (f32[160,320]{1,0:T(8,128)S(1)}, f32[160,320]{1,0:T(8,128)S(1)}, u32[]{:S(2)}, u32[]{:S(2)}) collective-permute-start(f32[160,320]{1,0:T(8,128)S(1)} %get-tuple-element.26.refs_1_.refs_2_), channel_id=1, source_target_pairs={{0,1},{1,0},{2,3},{3,2},{4,5},{5,4},{6,7},{7,6},{8,9},{9,8},{10,11... | collective-permute-start | bytes 614408 | tf_op jit(solution)/shard_map/ppermute | solution.py:422
  129.2 17.2 %collective-permute-start.30 = (f32[160,320]{1,0:T(8,128)S(1)}, f32[160,320]{1,0:T(8,128)S(1)}, u32[]{:S(2)}, u32[]{:S(2)}) collective-permute-start(f32[160,320]{1,0:T(8,128)S(1)} %get-tuple-element.40), channel_id=1, source_target_pairs={{0,3},{1,2},{2,1},{3,0},{4,7},{5,6},{6,5},{7,4},{8,11},{9,10},{10,... | collective-permute-start | bytes 614408 | tf_op jit(solution)/shard_map/ppermute | solution.py:422
  (29 other events, 179.8 us)

commit v3 on v2

--- a/solution.py
+++ b/solution.py
@@ -539,7 +539,7 @@
 
         lead = after(lead, pieces[1])
         leads = [lead] + [snp_xor(lead, bits) for bits in range(1, n_snp)]
-        waits = [[], [side], [pieces[1], sides[1]], leads[1:] + [moved[2]]]
+        waits = [[], [side], [sides[1]], []]
         for k in range(1, PANEL // BLOCK):
             inv, *more = factor_step(place, [square], PANEL - k * BLOCK, waits[k])
             inverses.append(inv)

time: 150 us -> 145 us (0.967)
  waiting for transfers between devices: 66.7 us -> 60.8 us
    ppermute x5, waiting for transfers between devices: 16.6 us -> 12.4 us  [snp_xor(): return lax.ppermute(x, 'snp', [(s, s ^ bits) for s in range(n_snp)])]
    ppermute x27, waiting for transfers between devices: 49.9 us -> 48.2 us  [rows_xor(): return lax.ppermute(x, 'rows', [(r, r ^ bits) for r in range(n_rows)])]
  transfers between devices with their start and end apart: 33 -> 33, of which waited for: 17 -> 19; matrix products, arithmetic and copies ran while one was open for 3% -> 3% of each run, Pallas kernels for 26% -> 26%
where the time goes in v3:
time: 145 us; the launch traced here: 144 us
  waiting for transfers between devices  60.8 us (42%)
  Pallas kernels  42 us (29%)
  starting transfers between devices  31.8 us (22%)
  other arithmetic  6.4 us (4%)
  between operations  2.31 us (2%)
    ppermute x27, waiting for transfers between devices, rows_xor(): return lax.ppermute(x, 'rows', [(r, r ^ bits) for r in range(n_rows)])  48.2 us
    pallas_call x4, Pallas kernels, factor_step(): pl.pallas_call(kernel, out_shape=out_shape, in_specs=[SMEM] + [VMEM] * n_...  22.4 us
    ppermute x27, starting transfers between devices, rows_xor(): return lax.ppermute(x, 'rows', [(r, r ^ bits) for r in range(n_rows)])  20.6 us
    ppermute x5, waiting for transfers between devices, snp_xor(): return lax.ppermute(x, 'snp', [(s, s ^ bits) for s in range(n_snp)])  12.4 us
    ppermute x5, starting transfers between devices, snp_xor(): return lax.ppermute(x, 'snp', [(s, s ^ bits) for s in range(n_snp)])  7.77 us
    pallas_call x2, Pallas kernels, head_products(): pl.pallas_call(functools.partial(head_kernel, len(left), sizes), out_shap...  5.48 us
    pallas_call x1, Pallas kernels, solve(): pl.pallas_call(functools.partial(solve_kernel, len(inverses), len(lead)),...  4.4 us
    select_n x3, other arithmetic, select_order(): jnp.where(swap, blocks[k ^ bit], blocks[k])  3.84 us
  transfers between devices with their start and end apart: 33, of which 19 were waited for; matrix products, arithmetic and copies ran while one was open for 3% of the time, Pallas kernels for 26%

profile of v3, /device:TPU:0, one launch (start us, length us, event | category | flops | bytes accessed | tf_op | source)
XLA Modules:
  0.0 144.5 jit_solution(2135702658554102483)
XLA Ops:
  2.2 3.0 %collective-permute-start.1 = (f32[2,1536]{1,0:T(2,128)S(1)}, f32[2,1536]{1,0:T(2,128)S(1)}, u32[]{:S(2)}, u32[]{:S(2)}) collective-permute-start(f32[2,1536]{1,0:T(2,128)S(1)} %pad_maximum_fusion), channel_id=1, source_target_pairs={{0,2},{1,3},{2,0},{3,1},{4,6},{5,7},{6,4},{7,5},{8,10},{9,11},{10,... | collective-permute-start | bytes 36872 | tf_op jit(solution)/shard_map/ppermute | solution.py:422
  8.4 3.7 %collective-permute-start.5 = (f32[2,1536]{1,0:T(2,128)S(1)}, f32[2,1536]{1,0:T(2,128)S(1)}, u32[]{:S(2)}, u32[]{:S(2)}) collective-permute-start(f32[2,1536]{1,0:T(2,128)S(1)} %add_add_fusion.1), channel_id=1, source_target_pairs={{0,12},{1,13},{2,14},{3,15},{4,8},{5,9},{6,10},{7,11},{8,4},{9,5},... | collective-permute-start | bytes 36872 | tf_op jit(solution)/shard_map/ppermute | solution.py:422
  12.9 3.4 %collective-permute-start.7 = (f32[160,512]{1,0:T(8,128)S(1)}, f32[160,512]{1,0:T(8,128)S(1)}, u32[]{:S(2)}, u32[]{:S(2)}) collective-permute-start(f32[160,512]{1,0:T(8,128)S(1)} %slice.11), channel_id=1, source_target_pairs={{0,16},{1,17},{2,18},{3,19},{4,20},{5,21},{6,22},{7,23},{8,24},{9,... | collective-permute-start | bytes 983048 | tf_op jit(solution)/shard_map/ppermute | solution.py:430
  18.5 2.9 %collective-permute-start.6 = (bf16[160,1536]{1,0:T(8,128)(2,1)S(1)}, bf16[160,1536]{1,0:T(8,128)(2,1)S(1)}, u32[]{:S(2)}, u32[]{:S(2)}) collective-permute-start(bf16[160,1536]{1,0:T(8,128)(2,1)S(1)} %select_convert_fusion.refs_0_), channel_id=1, source_target_pairs={{0,8},{1,9},{2,10},{3,11},{4,12},{5,13},{6,14},{7,15},{8,0},{9,1},... | collective-permute-start | bytes 1474568 | tf_op jit(solution)/shard_map/ppermute | solution.py:422
  22.4 16.9 %collective-permute-done.8.refs_2_ = bf16[160,1536]{1,0:T(8,128)(2,1)S(1)} collective-permute-done((bf16[160,1536]{1,0:T(8,128)(2,1)S(1)}, bf16[160,1536]{1,0:T(8,128)(2,1)S(1)}, u32[]{:S(2)}, u32[]{:S(2)}) %collective-permute-start.8) | collective-permute-done | bytes 491552 | tf_op jit(solution)/shard_map/ppermute | solution.py:422
  39.3 2.4 %collective-permute-done.6.refs_0_ = bf16[160,1536]{1,0:T(8,128)(2,1)S(1)} collective-permute-done((bf16[160,1536]{1,0:T(8,128)(2,1)S(1)}, bf16[160,1536]{1,0:T(8,128)(2,1)S(1)}, u32[]{:S(2)}, u32[]{:S(2)}) %collective-permute-start.6) | collective-permute-done | bytes 491552 | tf_op jit(solution)/shard_map/ppermute | solution.py:422
  42.5 11.3 %collective-permute-done.9.refs_0_ = bf16[160,1536]{1,0:T(8,128)(2,1)S(1)} collective-permute-done((bf16[160,1536]{1,0:T(8,128)(2,1)S(1)}, bf16[160,1536]{1,0:T(8,128)(2,1)S(1)}, u32[]{:S(2)}, u32[]{:S(2)}) %collective-permute-start.9) | collective-permute-done | bytes 491552 | tf_op jit(solution)/shard_map/ppermute | solution.py:422
  53.8 2.4 %collective-permute-start.13 = (f32[160,512]{1,0:T(8,128)S(1)}, f32[160,512]{1,0:T(8,128)S(1)}, u32[]{:S(2)}, u32[]{:S(2)}) collective-permute-start(f32[160,512]{1,0:T(8,128)S(1)} %shard_map.43), channel_id=1, source_target_pairs={{0,4},{1,5},{2,6},{3,7},{4,0},{5,1},{6,2},{7,3},{8,12},{9,13},{10,... | collective-permute-start | bytes 983048 | tf_op jit(solution)/shard_map/ppermute | solution.py:422
  62.3 2.8 %collective-permute-done.14.refs_2_ = f32[160,512]{1,0:T(8,128)} collective-permute-done((f32[160,512]{1,0:T(8,128)S(1)}, f32[160,512]{1,0:T(8,128)}, u32[]{:S(2)}, u32[]{:S(2)}) %collective-permute-start.14) | collective-permute-done | bytes 327712 | tf_op jit(solution)/shard_map/ppermute | solution.py:422
  68.5 2.7 %shard_map.47.refs_8_.refs_0_ = f32[168,512]{1,0:T(8,128)S(1)} custom-call(s32[2]{0:T(128)S(1)} %pad_add_fusion.place.refs_0_, f32[1]{0:T(128)} %bitcast.2.scale, bf16[160,1536]{1,0:T(8,128)(2,1)S(1)} %select_select_fusion.refs_1_.first.refs_0_.refs_4_, bf16[160,1536]{1,0:T(8,128)(2,1)S(1)} %select_select_fusion.refs_1_.first.refs_0_.refs_4_, ...), custom_call_target="tpu_custom_call" | custom-call | flops 251658240 | bytes 131072 | tf_op jit(solution)/shard_map/pallas_call | solution.py:227
  73.0 3.5 %shard_map.48 = (f32[320,512]{1,0:T(8,128)S(1)}, f32[160,512]{1,0:T(8,128)S(1)}, f32[160,512]{1,0:T(8,128)S(1)}) custom-call(s32[2]{0:T(128)S(1)} %pad_add_fusion.place.refs_0_, bf16[160,1536]{1,0:T(8,128)(2,1)S(1)} %copy-done.1, bf16[160,1536]{1,0:T(8,128)(2,1)S(1)} %copy-done, bf16[160,1536]{1,0:T(8,128)(2,1)S(1)} %copy-done.5, ...), custom_call_target="tpu_custom_call" | custom-call | flops 1006632960 | bytes 131072 | tf_op jit(solution)/shard_map/pallas_call | solution.py:295
  79.1 2.3 %collective-permute-done.18.refs_1_ = f32[168,512]{1,0:T(8,128)S(1)} collective-permute-done((f32[168,512]{1,0:T(8,128)S(1)}, f32[168,512]{1,0:T(8,128)S(1)}, u32[]{:S(2)}, u32[]{:S(2)}) %collective-permute-start.18) | collective-permute-done | bytes 344096 | tf_op jit(solution)/shard_map/ppermute | solution.py:425
  84.9 2.0 %shard_map.54.refs_0_.refs_1_ = f32[160,512]{1,0:T(8,128)S(1)} custom-call(s32[2]{0:T(128)S(1)} %pad_add_fusion.place.refs_0_, bf16[160,1536]{1,0:T(8,128)(2,1)S(1)} %select_convert_fusion.refs_0_, bf16[160,1536]{1,0:T(8,128)(2,1)S(1)} %select_select_fusion.refs_1_.first.refs_0_.refs_4_, bf16[160,1536]{1,0:T(8,128)(2,1)} %collective-permute-done.11.refs_1_.refs_5_.refs_2_, ...), custom_call_target="tpu_custom_call" | custom-call | flops 251658240 | bytes 131072 | tf_op jit(solution)/shard_map/pallas_call | solution.py:295
  86.9 3.8 %collective-permute-done.24.refs_0_ = f32[160,512]{1,0:T(8,128)S(1)} collective-permute-done((f32[160,512]{1,0:T(8,128)S(1)}, f32[160,512]{1,0:T(8,128)S(1)}, u32[]{:S(2)}, u32[]{:S(2)}) %collective-permute-start.24) | collective-permute-done | bytes 327712 | tf_op jit(solution)/shard_map/ppermute | solution.py:422
  93.7 6.2 %shard_map.59 = (f32[128,128]{1,0:T(8,128)S(1)}, f32[384,128]{1,0:T(8,128)S(1)}, f32[384,384]{1,0:T(8,128)S(1)}) custom-call(s32[2]{0:T(128)S(1)} %pad_add_fusion.place.refs_0_, f32[160,512]{1,0:T(8,128)S(1)} %shard_map.53.refs_5_.refs_1_, f32[160,512]{1,0:T(8,128)S(1)} %collective-permute-done.23.refs_2_, f32[160,512]{1,0:T(8,128)S(1)} %shard_map.58.refs_3_, ...), custom_call_target="tpu_custom_call" | custom-call | flops 3500000000 | bytes 131072 | tf_op jit(solution)/shard_map/pallas_call | solution.py:157
  100.0 2.3 %collective-permute-done.26.refs_1_ = f32[160,512]{1,0:T(8,128)S(1)} collective-permute-done((f32[160,512]{1,0:T(8,128)S(1)}, f32[160,512]{1,0:T(8,128)S(1)}, u32[]{:S(2)}, u32[]{:S(2)}) %collective-permute-start.26) | collective-permute-done | bytes 327712 | tf_op jit(solution)/shard_map/ppermute | solution.py:425
  104.3 5.9 %shard_map.61 = (f32[128,128]{1,0:T(8,128)S(1)}, f32[256,128]{1,0:T(8,128)S(1)}, f32[256,256]{1,0:T(8,128)S(1)}) custom-call(s32[2]{0:T(128)S(1)} %pad_add_fusion.place.refs_0_, f32[384,384]{1,0:T(8,128)S(1)} %get-tuple-element.28.refs_1_, f32[320,512]{1,0:T(8,128)S(1)} %shard_map.60.refs_2_.refs_4_), custom_call_target="tpu_custom_call" | custom-call | flops 3500000000 | bytes 131072 | tf_op jit(solution)/shard_map/pallas_call | solution.py:157
  110.3 5.7 %shard_map.62 = (f32[128,128]{1,0:T(8,128)S(1)}, f32[128,128]{1,0:T(8,128)S(1)}, f32[128,128]{1,0:T(8,128)S(1)}) custom-call(s32[2]{0:T(128)S(1)} %pad_add_fusion.place.refs_0_, f32[256,256]{1,0:T(8,128)S(1)} %get-tuple-element.31.refs_1_, f32[320,512]{1,0:T(8,128)S(1)} %collective-permute-done.27.refs_2_.refs_5_), custom_call_target="tpu_custom_call" | custom-call | flops 3500000000 | bytes 131072 | tf_op jit(solution)/shard_map/pallas_call | solution.py:157
  116.0 4.8 %collective-permute-done.31.refs_0_ = f32[320,512]{1,0:T(8,128)S(1)} collective-permute-done((f32[320,512]{1,0:T(8,128)S(1)}, f32[320,512]{1,0:T(8,128)S(1)}, u32[]{:S(2)}, u32[]{:S(2)}) %collective-permute-start.31) | collective-permute-done | bytes 655392 | tf_op jit(solution)/shard_map/ppermute | solution.py:422
  120.8 2.4 %collective-permute-done.21.refs_6_ = f32[320,640]{1,0:T(8,128)S(1)} collective-permute-done((f32[320,640]{1,0:T(8,128)S(1)}, f32[320,640]{1,0:T(8,128)S(1)}, u32[]{:S(2)}, u32[]{:S(2)}) %collective-permute-start.21) | collective-permute-done | bytes 819232 | tf_op jit(solution)/shard_map/ppermute | solution.py:425
  128.0 4.5 %shard_map.63.refs_5_ = f32[128,128]{1,0:T(8,128)S(1)} custom-call(s32[2]{0:T(128)S(1)} %pad_add_fusion.place.refs_0_, f32[128,128]{1,0:T(8,128)S(1)} %get-tuple-element.33.refs_1_), custom_call_target="tpu_custom_call" | custom-call | flops 3500000000 | bytes 131072 | tf_op jit(solution)/shard_map/pallas_call | solution.py:157
  132.5 4.0 %collective-permute-done.22.refs_1_ = f32[160,512]{1,0:T(8,128)S(1)} collective-permute-done((f32[160,512]{1,0:T(8,128)S(1)}, f32[160,512]{1,0:T(8,128)S(1)}, u32[]{:S(2)}, u32[]{:S(2)}) %collective-permute-start.22) | collective-permute-done | bytes 327712 | tf_op jit(solution)/shard_map/ppermute | solution.py:425
  136.6 4.4 %shard_map.64 = (f32[160,512]{1,0:T(8,128)}, f32[160,512]{1,0:T(8,128)S(1)}) custom-call(f32[160,512]{1,0:T(8,128)S(1)} %select_add_fusion.refs_1_.rel, f32[8,128]{1,0:T(8,128)S(1)} %get-tuple-element.23.scale, f32[160,512]{1,0:T(8,128)S(1)} %shard_map.57.refs_0_, f32[160,512]{1,0:T(8,128)S(1)} %collective-permute-done.22.refs_1_, ...), custom_call_target="tpu_custom_call" | custom-call | flops 167772160 | bytes 131072 | tf_op jit(solution)/shard_map/pallas_call | solution.py:195
  141.0 3.5 %shard_map.66 = f32[160,1280]{1,0:T(8,128)} custom-call(s32[2]{0:T(128)S(1)} %pad_add_fusion.place.refs_0_, f32[8,128]{1,0:T(8,128)S(1)} %get-tuple-element.23.scale, f32[160,1280]{1,0:T(8,128)S(1)} %copy-done.11, f32[160,512]{1,0:T(8,128)S(1)} %get-tuple-element.37.weights, f32[160,320]{1,0:T(8,128)S(1)} %get-tuple-element.38.refs_0_, ...), custom_call_target="tpu_custom_call" | custom-call | flops 209715200 | bytes 131072 | tf_op jit(solution)/shard_map/pallas_call | solution.py:376
  (124 shorter events, 35.5 us)
Async XLA Ops:
  8.4 7.9 %collective-permute-start.5 = (f32[2,1536]{1,0:T(2,128)S(1)}, f32[2,1536]{1,0:T(2,128)S(1)}, u32[]{:S(2)}, u32[]{:S(2)}) collective-permute-start(f32[2,1536]{1,0:T(2,128)S(1)} %add_add_fusion.1), channel_id=1, source_target_pairs={{0,12},{1,13},{2,14},{3,15},{4,8},{5,9},{6,10},{7,11},{8,4},{9,5},... | collective-permute-start | bytes 36872 | tf_op jit(solution)/shard_map/ppermute | solution.py:422
  12.9 9.4 %collective-permute-start.7 = (f32[160,512]{1,0:T(8,128)S(1)}, f32[160,512]{1,0:T(8,128)S(1)}, u32[]{:S(2)}, u32[]{:S(2)}) collective-permute-start(f32[160,512]{1,0:T(8,128)S(1)} %slice.11), channel_id=1, source_target_pairs={{0,16},{1,17},{2,18},{3,19},{4,20},{5,21},{6,22},{7,23},{8,24},{9,... | collective-permute-start | bytes 983048 | tf_op jit(solution)/shard_map/ppermute | solution.py:430
  17.5 21.8 %collective-permute-start.8 = (bf16[160,1536]{1,0:T(8,128)(2,1)S(1)}, bf16[160,1536]{1,0:T(8,128)(2,1)S(1)}, u32[]{:S(2)}, u32[]{:S(2)}) collective-permute-start(bf16[160,1536]{1,0:T(8,128)(2,1)S(1)} %select_convert_fusion.refs_0_), channel_id=1, source_target_pairs={{0,4},{1,5},{2,6},{3,7},{4,0},{5,1},{6,2},{7,3},{8,12},{9,13},{10,... | collective-permute-start | bytes 1474568 | tf_op jit(solution)/shard_map/ppermute | solution.py:422
  18.5 23.1 %collective-permute-start.6 = (bf16[160,1536]{1,0:T(8,128)(2,1)S(1)}, bf16[160,1536]{1,0:T(8,128)(2,1)S(1)}, u32[]{:S(2)}, u32[]{:S(2)}) collective-permute-start(bf16[160,1536]{1,0:T(8,128)(2,1)S(1)} %select_convert_fusion.refs_0_), channel_id=1, source_target_pairs={{0,8},{1,9},{2,10},{3,11},{4,12},{5,13},{6,14},{7,15},{8,0},{9,1},... | collective-permute-start | bytes 1474568 | tf_op jit(solution)/shard_map/ppermute | solution.py:422
  21.4 20.5 %collective-permute-start.10 = (bf16[160,1536]{1,0:T(8,128)(2,1)S(1)}, bf16[160,1536]{1,0:T(8,128)(2,1)S(1)}, u32[]{:S(2)}, u32[]{:S(2)}) collective-permute-start(bf16[160,1536]{1,0:T(8,128)(2,1)S(1)} %select_convert_fusion.refs_0_), channel_id=1, source_target_pairs={{0,2},{1,3},{2,0},{3,1},{4,6},{5,7},{6,4},{7,5},{8,10},{9,11},{10,... | collective-permute-start | bytes 1474568 | tf_op jit(solution)/shard_map/ppermute | solution.py:422
  41.6 12.1 %collective-permute-start.9 = (bf16[160,1536]{1,0:T(8,128)(2,1)S(1)}, bf16[160,1536]{1,0:T(8,128)(2,1)S(1)}, u32[]{:S(2)}, u32[]{:S(2)}) collective-permute-start(bf16[160,1536]{1,0:T(8,128)(2,1)S(1)} %shard_map.41), channel_id=1, source_target_pairs={{0,4},{1,5},{2,6},{3,7},{4,0},{5,1},{6,2},{7,3},{8,12},{9,13},{10,... | collective-permute-start | bytes 1474568 | tf_op jit(solution)/shard_map/ppermute | solution.py:422
  41.9 19.0 %collective-permute-start.15 = (bf16[160,1536]{1,0:T(8,128)(2,1)S(1)}, bf16[160,1536]{1,0:T(8,128)(2,1)S(1)}, u32[]{:S(2)}, u32[]{:S(2)}) collective-permute-start(bf16[160,1536]{1,0:T(8,128)(2,1)S(1)} %select_convert_fusion.refs_0_), channel_id=1, source_target_pairs={{0,1},{1,0},{2,3},{3,2},{4,5},{5,4},{6,7},{7,6},{8,9},{9,8},{10,11... | collective-permute-start | bytes 1474568 | tf_op jit(solution)/shard_map/ppermute | solution.py:422
  41.9 19.0 %collective-permute-start.16 = (bf16[160,1536]{1,0:T(8,128)(2,1)S(1)}, bf16[160,1536]{1,0:T(8,128)(2,1)S(1)}, u32[]{:S(2)}, u32[]{:S(2)}) collective-permute-start(bf16[160,1536]{1,0:T(8,128)(2,1)S(1)} %collective-permute-done.10.refs_1_.refs_2_), channel_id=1, source_target_pairs={{0,1},{1,0},{2,3},{3,2},{4,5},{5,4},{6,7},{7,6},{8,9},{9,8},{10,11... | collective-permute-start | bytes 1474568 | tf_op jit(solution)/shard_map/ppermute | solution.py:422
  53.8 11.3 %collective-permute-start.14 = (f32[160,512]{1,0:T(8,128)S(1)}, f32[160,512]{1,0:T(8,128)}, u32[]{:S(2)}, u32[]{:S(2)}) collective-permute-start(f32[160,512]{1,0:T(8,128)S(1)} %shard_map.43), channel_id=1, source_target_pairs={{0,8},{1,9},{2,10},{3,11},{4,12},{5,13},{6,14},{7,15},{8,0},{9,1},... | collective-permute-start | bytes 983048 | tf_op jit(solution)/shard_map/ppermute | solution.py:422
  53.8 11.3 %collective-permute-start.13 = (f32[160,512]{1,0:T(8,128)S(1)}, f32[160,512]{1,0:T(8,128)S(1)}, u32[]{:S(2)}, u32[]{:S(2)}) collective-permute-start(f32[160,512]{1,0:T(8,128)S(1)} %shard_map.43), channel_id=1, source_target_pairs={{0,4},{1,5},{2,6},{3,7},{4,0},{5,1},{6,2},{7,3},{8,12},{9,13},{10,... | collective-permute-start | bytes 983048 | tf_op jit(solution)/shard_map/ppermute | solution.py:422
  57.6 8.9 %collective-permute-start.12 = (bf16[160,1536]{1,0:T(8,128)(2,1)S(1)}, bf16[160,1536]{1,0:T(8,128)(2,1)S(1)}, u32[]{:S(2)}, u32[]{:S(2)}) collective-permute-start(bf16[160,1536]{1,0:T(8,128)(2,1)S(1)} %select_select_fusion.refs_1_.first.refs_0_.refs_4_), channel_id=1, source_target_pairs={{0,2},{1,3},{2,0},{3,1},{4,6},{5,7},{6,4},{7,5},{8,10},{9,11},{10,... | collective-permute-start | bytes 1474568 | tf_op jit(solution)/shard_map/ppermute | solution.py:422
  66.5 10.4 %collective-permute-start.19 = (f32[160,512]{1,0:T(8,128)}, f32[160,512]{1,0:T(8,128)}, u32[]{:S(2)}, u32[]{:S(2)}) collective-permute-start(f32[160,512]{1,0:T(8,128)} %collective-permute-done.14.refs_2_), channel_id=1, source_target_pairs={{0,4},{1,5},{2,6},{3,7},{4,0},{5,1},{6,2},{7,3},{8,12},{9,13},{10,... | collective-permute-start | bytes 983048 | tf_op jit(solution)/shard_map/ppermute | solution.py:422
  71.3 10.2 %collective-permute-start.18 = (f32[168,512]{1,0:T(8,128)S(1)}, f32[168,512]{1,0:T(8,128)S(1)}, u32[]{:S(2)}, u32[]{:S(2)}) collective-permute-start(f32[168,512]{1,0:T(8,128)S(1)} %shard_map.47.refs_8_.refs_0_), channel_id=1, source_target_pairs={{0,16},{16,0},{1,17},{17,1},{2,18},{18,2},{3,19},{19,3},{4,20},{20... | collective-permute-start | bytes 1032200 | tf_op jit(solution)/shard_map/ppermute | solution.py:425
  81.5 9.1 %collective-permute-start.24 = (f32[160,512]{1,0:T(8,128)S(1)}, f32[160,512]{1,0:T(8,128)S(1)}, u32[]{:S(2)}, u32[]{:S(2)}) collective-permute-start(f32[160,512]{1,0:T(8,128)S(1)} %shard_map.53.refs_5_.refs_1_), channel_id=1, source_target_pairs={{0,2},{1,3},{2,0},{3,1},{4,6},{5,7},{6,4},{7,5},{8,10},{9,11},{10,... | collective-permute-start | bytes 983048 | tf_op jit(solution)/shard_map/ppermute | solution.py:422
  83.2 9.0 %collective-permute-start.20 = (f32[160,512]{1,0:T(8,128)S(1)}, f32[160,512]{1,0:T(8,128)S(1)}, u32[]{:S(2)}, u32[]{:S(2)}) collective-permute-start(f32[160,512]{1,0:T(8,128)S(1)} %shard_map.51.refs_1_), channel_id=1, source_target_pairs={{0,16},{16,0},{1,17},{17,1},{2,18},{18,2},{3,19},{19,3},{4,20},{20... | collective-permute-start | bytes 983048 | tf_op jit(solution)/shard_map/ppermute | solution.py:425
  84.9 8.6 %collective-permute-start.23 = (f32[160,512]{1,0:T(8,128)S(1)}, f32[160,512]{1,0:T(8,128)S(1)}, u32[]{:S(2)}, u32[]{:S(2)}) collective-permute-start(f32[160,512]{1,0:T(8,128)S(1)} %shard_map.53.refs_5_.refs_1_), channel_id=1, source_target_pairs={{0,1},{1,0},{2,3},{3,2},{4,5},{5,4},{6,7},{7,6},{8,9},{9,8},{10,11... | collective-permute-start | bytes 983048 | tf_op jit(solution)/shard_map/ppermute | solution.py:422
  92.1 10.1 %collective-permute-start.26 = (f32[160,512]{1,0:T(8,128)S(1)}, f32[160,512]{1,0:T(8,128)S(1)}, u32[]{:S(2)}, u32[]{:S(2)}) collective-permute-start(f32[160,512]{1,0:T(8,128)S(1)} %shard_map.52.refs_2_), channel_id=1, source_target_pairs={{0,16},{16,0},{1,17},{17,1},{2,18},{18,2},{3,19},{19,3},{4,20},{20... | collective-permute-start | bytes 983048 | tf_op jit(solution)/shard_map/ppermute | solution.py:425
  102.5 20.7 %collective-permute-start.21 = (f32[320,640]{1,0:T(8,128)S(1)}, f32[320,640]{1,0:T(8,128)S(1)}, u32[]{:S(2)}, u32[]{:S(2)}) collective-permute-start(f32[320,640]{1,0:T(8,128)S(1)} %shard_map.55), channel_id=1, source_target_pairs={{0,16},{16,0},{1,17},{17,1},{2,18},{18,2},{3,19},{19,3},{4,20},{20... | collective-permute-start | bytes 2457608 | tf_op jit(solution)/shard_map/ppermute | solution.py:425
  104.0 16.8 %collective-permute-start.31 = (f32[320,512]{1,0:T(8,128)S(1)}, f32[320,512]{1,0:T(8,128)S(1)}, u32[]{:S(2)}, u32[]{:S(2)}) collective-permute-start(f32[320,512]{1,0:T(8,128)S(1)} %shard_map.60.refs_2_.refs_4_), channel_id=1, source_target_pairs={{0,2},{1,3},{2,0},{3,1},{4,6},{5,7},{6,4},{7,5},{8,10},{9,11},{10,... | collective-permute-start | bytes 1966088 | tf_op jit(solution)/shard_map/ppermute | solution.py:422
  120.8 20.2 %collective-permute-start.32 = (f32[320,512]{1,0:T(8,128)S(1)}, f32[320,512]{1,0:T(8,128)S(1)}, u32[]{:S(2)}, u32[]{:S(2)}) collective-permute-start(f32[320,512]{1,0:T(8,128)S(1)} %shard_map.65.refs_6_), channel_id=1, source_target_pairs={{0,1},{1,0},{2,3},{3,2},{4,5},{5,4},{6,7},{7,6},{8,9},{9,8},{10,11... | collective-permute-start | bytes 1966088 | tf_op jit(solution)/shard_map/ppermute | solution.py:422
  124.6 16.3 %collective-permute-start.28 = (f32[160,320]{1,0:T(8,128)S(1)}, f32[160,320]{1,0:T(8,128)S(1)}, u32[]{:S(2)}, u32[]{:S(2)}) collective-permute-start(f32[160,320]{1,0:T(8,128)S(1)} %get-tuple-element.26.refs_1_), channel_id=1, source_target_pairs={{0,1},{1,0},{2,3},{3,2},{4,5},{5,4},{6,7},{7,6},{8,9},{9,8},{10,11... | collective-permute-start | bytes 614408 | tf_op jit(solution)/shard_map/ppermute | solution.py:422
  124.7 16.2 %collective-permute-start.29 = (f32[160,320]{1,0:T(8,128)S(1)}, f32[160,320]{1,0:T(8,128)S(1)}, u32[]{:S(2)}, u32[]{:S(2)}) collective-permute-start(f32[160,320]{1,0:T(8,128)S(1)} %get-tuple-element.39), channel_id=1, source_target_pairs={{0,2},{1,3},{2,0},{3,1},{4,6},{5,7},{6,4},{7,5},{8,10},{9,11},{10,... | collective-permute-start | bytes 614408 | tf_op jit(solution)/shard_map/ppermute | solution.py:422
  125.2 15.8 %collective-permute-start.30 = (f32[160,320]{1,0:T(8,128)S(1)}, f32[160,320]{1,0:T(8,128)S(1)}, u32[]{:S(2)}, u32[]{:S(2)}) collective-permute-start(f32[160,320]{1,0:T(8,128)S(1)} %get-tuple-element.40), channel_id=1, source_target_pairs={{0,3},{1,2},{2,1},{3,0},{4,7},{5,6},{6,5},{7,4},{8,11},{9,10},{10,... | collective-permute-start | bytes 614408 | tf_op jit(solution)/shard_map/ppermute | solution.py:422
  126.6 10.0 %collective-permute-start.22 = (f32[160,512]{1,0:T(8,128)S(1)}, f32[160,512]{1,0:T(8,128)S(1)}, u32[]{:S(2)}, u32[]{:S(2)}) collective-permute-start(f32[160,512]{1,0:T(8,128)S(1)} %shard_map.57.refs_0_), channel_id=1, source_target_pairs={{0,16},{16,0},{1,17},{17,1},{2,18},{18,2},{3,19},{19,3},{4,20},{20... | collective-permute-start | bytes 983048 | tf_op jit(solution)/shard_map/ppermute | solution.py:425
  (29 other events, 151.0 us)
